TPU v7x, 256 devices: a whole 4x4x8 slice. The times are simulated.
256 devices in a mesh: row: 64 (over x, y_hi, z), col: 4 (over y_lo, core).
Axes of the slice: x: 4, y: 4 (y_hi: 2, y_lo: 2; y = y_hi * 2 + y_lo), z: 8, core: 2. Of those that a mesh axis runs over, the one named last changes fastest.
Arguments:
- east_flow: float32 [768, 128, 768], P('row', 'col'), may hold values from -8 to 8
- north_flow: float32 [768, 128, 768], P('row', 'col'), may hold values from -8 to 8
- upward_flow: float32 [768, 128, 768], P('row', 'col'), may hold values from -8 to 8
- solid: int32 [768, 128, 768], P('row', 'col'), may hold values 0 or 1
- inflow_cells: int32 [4096], replicated, may hold values from 0 to 75497471, as said below
- inflow_speed: float32 [4096], replicated, may hold values from 0.5 to 2
Outputs:
- projected_east: float32 [768, 128, 768], P('row', 'col')
- projected_north: float32 [768, 128, 768], P('row', 'col')
- projected_upward: float32 [768, 128, 768], P('row', 'col')
Inputs may be any that keep to these rules, and one draw needn't show every extreme that they name: `inflow_cells`: Distinct; the k-th index lies in [k * 768 * 128 * 768 / 4096, (k + 1) * 768 * 128 * 768 / 4096).
All inputs are finite; a program needn't handle non-finite values. No bound on the sum of `solid` on one device may be relied on, other than what follows from the above.
Results may differ from a plain program's by a relative error of at most 0.0003.
Values sent between devices are 32-bit elements; how exact they have to be, the bound alone decides.
No kernel may reach another device: no remote copies, remote signals or barrier semaphores. Data moves between devices by JAX's collectives and lax.ppermute only.
A program may use at most 128 MiB of HBM per device.

v0:
```python
import math

import jax
import jax.numpy as jnp
from jax import lax
from jax.sharding import PartitionSpec as P

COEF_ALPHA = 1.0 / 3.0
COEF_A = 14.0 / 9.0
COEF_B = 1.0 / 9.0
precise = lax.Precision.HIGHEST


def wave_numbers(length):
    indices = jnp.arange(length, dtype=jnp.int32)
    phases = 2.0 * math.pi / length * indices.astype(jnp.float32)
    modified = (COEF_A * jnp.sin(phases) + 0.5 * COEF_B * jnp.sin(2.0 * phases)) / (
        1.0 + 2.0 * COEF_ALPHA * jnp.cos(phases)
    )
    nulled = (indices == 0) | (2 * indices == length)
    return (jnp.where(nulled, 0.0, modified), nulled)


def angle_matrix(length):
    indices = jnp.arange(length, dtype=jnp.int32)
    product = indices[:, None] * indices[None, :] % length
    return 2.0 * math.pi / length * product.astype(jnp.float32)


def hartley_matrix(length):
    angles = angle_matrix(length)
    return jnp.cos(angles) + jnp.sin(angles)


def derivative_matrix(length):
    wavenumber, nulled = wave_numbers(length)
    first_row = jnp.dot(wavenumber, jnp.sin(angle_matrix(length)), precision=precise) / length
    tiled = jnp.tile(first_row, length + 1).reshape(length, length + 1)[:, :length]
    return jnp.roll(tiled[::-1], 1, axis=0)


def along_last(volume, matrix):
    return jnp.dot(volume, matrix.T, precision=precise)


def along_first(matrix, volume):
    return jnp.tensordot(matrix, volume, axes=1, precision=precise)


def inverse_factor(wavenumbers, nulls, normalizer):
    denominator = wavenumbers[0] ** 2 + wavenumbers[1] ** 2 + wavenumbers[2] ** 2
    nulled = nulls[0] & nulls[1] & nulls[2]
    return jnp.where(nulled, 0.0, -1.0 / jnp.where(nulled, 1.0, denominator)) / normalizer


def body(east_flow, north_flow, upward_flow, solid, inflow_cells, inflow_speed):
    row_count = lax.axis_size("row")
    col_count = lax.axis_size("col")
    row_place = lax.axis_index("row")
    col_place = lax.axis_index("col")
    north_local, upward_local, east_total = east_flow.shape
    north_total = north_local * row_count
    upward_total = upward_local * col_count
    east_local = east_total // row_count
    north_share = north_total // col_count
    plane_local = upward_local * east_local
    fluid = (1 - solid).astype(jnp.float32)
    masked_east = east_flow * fluid
    masked_north = north_flow * fluid
    plane_cells = upward_total * east_total
    cell_north = inflow_cells // plane_cells
    remainder = inflow_cells % plane_cells
    cell_upward = remainder // east_total
    cell_east = remainder % east_total
    local_north = cell_north - row_place * north_local
    local_upward = cell_upward - col_place * upward_local
    inside = (
        (local_north >= 0)
        & (local_north < north_local)
        & (local_upward >= 0)
        & (local_upward < upward_local)
    )
    local_cells = north_local * upward_local * east_total
    target = jnp.where(
        inside, (local_north * upward_local + local_upward) * east_total + cell_east, local_cells
    )
    masked_upward = (
        (upward_flow * fluid)
        .reshape(local_cells)
        .at[target]
        .set(inflow_speed, mode="drop")
        .reshape(east_flow.shape)
    )
    deriv_east = derivative_matrix(east_total)
    hartley_east = hartley_matrix(east_total)
    deriv_north = derivative_matrix(north_total)
    hartley_north = hartley_matrix(north_total)
    deriv_upward = derivative_matrix(upward_total)
    hartley_upward = hartley_matrix(upward_total)
    wave_east, null_east = wave_numbers(east_total)
    wave_north, null_north = wave_numbers(north_total)
    wave_upward, null_upward = wave_numbers(upward_total)
    normalizer = float(east_total * north_total * upward_total)
    wave_up_local = lax.dynamic_slice_in_dim(wave_upward, col_place * upward_local, upward_local)
    null_up_local = lax.dynamic_slice_in_dim(null_upward, col_place * upward_local, upward_local)
    div_east = along_last(masked_east, deriv_east)

    def to_north(volume):
        blocks = volume.reshape(north_local, upward_local, row_count, east_local)
        return jnp.transpose(blocks, (2, 0, 1, 3)).reshape(row_count, north_local, plane_local)

    def north_layout(member):
        return member.reshape(north_total, plane_local)

    def from_north(volume):
        return volume.reshape(row_count, north_local, plane_local)

    def east_layout(member):
        blocks = member.reshape(row_count, north_local, upward_local, east_local)
        return jnp.transpose(blocks, (1, 2, 0, 3)).reshape(north_local, upward_local, east_total)

    def to_upward(volume):
        return volume.reshape(col_count, north_share, plane_local)

    def upward_layout(member):
        blocks = member.reshape(col_count, north_share, upward_local, east_local)
        return jnp.transpose(blocks, (1, 3, 0, 2)).reshape(north_share, east_local, upward_total)

    def from_upward(volume):
        blocks = volume.reshape(north_share, east_local, col_count, upward_local)
        return jnp.transpose(blocks, (2, 0, 3, 1)).reshape(col_count, north_share, plane_local)

    arrived = (
        lax.all_to_all(to_north(masked_north), "row", split_axis=0, concat_axis=0, tiled=True),
        lax.all_to_all(to_north(masked_upward), "row", split_axis=0, concat_axis=0, tiled=True),
        lax.all_to_all(to_north(div_east), "row", split_axis=0, concat_axis=0, tiled=True),
    )
    north_y, upward_y, partial_value = [north_layout(member) for member in arrived]
    partial_value = partial_value + along_first(deriv_north, north_y)
    arrived = (
        lax.all_to_all(to_upward(upward_y), "col", split_axis=0, concat_axis=0, tiled=True),
        lax.all_to_all(to_upward(partial_value), "col", split_axis=0, concat_axis=0, tiled=True),
    )
    upward_z, partial_z = [upward_layout(member) for member in arrived]
    spectrum = along_last(partial_z + along_last(upward_z, deriv_upward), hartley_upward)
    returned = lax.all_to_all(from_upward(spectrum), "col", split_axis=0, concat_axis=0, tiled=True)
    spectrum = along_first(hartley_north, north_layout(returned))
    returned = lax.all_to_all(from_north(spectrum), "row", split_axis=0, concat_axis=0, tiled=True)
    spectrum = along_last(east_layout(returned), hartley_east)
    wave_north_local = lax.dynamic_slice_in_dim(wave_north, row_place * north_local, north_local)
    null_north_local = lax.dynamic_slice_in_dim(null_north, row_place * north_local, north_local)
    inverse = inverse_factor(
        (wave_north_local[:, None, None], wave_up_local[None, :, None], wave_east[None, None, :]),
        (null_north_local[:, None, None], null_up_local[None, :, None], null_east[None, None, :]),
        normalizer,
    )
    pressure = along_last(spectrum * inverse, hartley_east)
    arrived = lax.all_to_all(to_north(pressure), "row", split_axis=0, concat_axis=0, tiled=True)
    pressure = along_first(hartley_north, north_layout(arrived))
    arrived = lax.all_to_all(to_upward(pressure), "col", split_axis=0, concat_axis=0, tiled=True)
    pressure = along_last(upward_layout(arrived), hartley_upward)
    final_upward = upward_z - along_last(pressure, deriv_upward)
    returned = (
        lax.all_to_all(from_upward(pressure), "col", split_axis=0, concat_axis=0, tiled=True),
        lax.all_to_all(from_upward(final_upward), "col", split_axis=0, concat_axis=0, tiled=True),
    )
    pressure_y, final_upward_y = [north_layout(member) for member in returned]
    final_north = north_y - along_first(deriv_north, pressure_y)
    returned = (
        lax.all_to_all(from_north(pressure_y), "row", split_axis=0, concat_axis=0, tiled=True),
        lax.all_to_all(from_north(final_north), "row", split_axis=0, concat_axis=0, tiled=True),
        lax.all_to_all(from_north(final_upward_y), "row", split_axis=0, concat_axis=0, tiled=True),
    )
    pressure_x, projected_north, projected_upward = [east_layout(member) for member in returned]
    projected_east = masked_east - along_last(pressure_x, deriv_east)
    return (projected_east, projected_north, projected_upward)


def solution(mesh):
    in_specs = (
        P("row", "col", None),
        P("row", "col", None),
        P("row", "col", None),
        P("row", "col", None),
        P(),
        P(),
    )
    out_specs = (P("row", "col", None), P("row", "col", None), P("row", "col", None))
    return jax.shard_map(body, mesh=mesh, in_specs=in_specs, out_specs=out_specs, check_vma=False)
```

profile of v0, /device:TPU:1, one launch (start us, length us, event | category | flops | bytes accessed | tf_op | source)
XLA Modules:
  0.0 824.9 jit_solution(213322281742924539)
XLA Ops:
  1.3 10.3 %fusion.65 = f32[768]{0:T(1024)S(1)} fusion(f32[768,1]{0,1:T(1,128)S(1)} %reshape.372), kind=kOutput, calls=%fused_computation.71 | convolution fusion | flops 12386304 | bytes 6144 | tf_op jit(solution)/shard_map/dot_general | solution.py:37
  23.4 16.6 %slice.35 = f32[767,768]{1,0:T(8,128)S(1)} reverse(f32[767,768]{1,0:T(8,128)} %slice.40), dimensions={0} | reverse | bytes 4712448 | tf_op jit(solution)/shard_map/jit(_roll_static)/slice | solution.py:39
  40.0 14.1 %fusion.12 = f32[12,32,768]{1,2,0:T(8,128)} fusion(f32[767,768]{1,0:T(8,128)S(1)} %slice.35, f32[1,768]{1,0:T(1,128)S(1)} %slice.39, f32[12,32,768]{2,1,0:T(8,128)} %param.6, s32[12,32,768]{2,1,0:T(8,128)S(1)} %copy-done.2), kind=kOutput, calls=%fused_computation.17 | convolution fusion | flops 2719383552 | bytes 5898240 | tf_op jit(solution)/shard_map/dot_general | solution.py:43
  74.4 15.4 %all-to-all-start = ((f32[64,12,384]{2,1,0:T(8,128)}), f32[64,12,384]{2,1,0:T(8,128)}, u32[]{:S(2)}, u32[]{:S(2)}) async-start(f32[64,12,384]{2,1,0:T(8,128)} %copy.97), calls=%async_computation | async-start | bytes 3145728 | tf_op jit(solution)/shard_map/all_to_all | solution.py:136
  117.4 10.9 %all-to-all-done = f32[64,12,384]{2,1,0:T(8,128)} async-done(((f32[64,12,384]{2,1,0:T(8,128)}), f32[64,12,384]{2,1,0:T(8,128)}, u32[]{:S(2)}, u32[]{:S(2)}) %all-to-all-start) | async-done | bytes 1179680 | tf_op jit(solution)/shard_map/all_to_all | solution.py:136
  139.2 16.2 %scatter_fusion = f32[294912]{0:T(1024)S(1)} fusion(f32[294912]{0:T(1024)S(1)} %reshape.337, s32[4096]{0:T(1024)S(1)} %compare_select_fusion, f32[4096]{0:T(1024)} %param.11), kind=kCustom, calls=%fused_computation | custom fusion | bytes 65536 | tf_op jit(solution)/shard_map/scatter | solution.py:91
  155.4 15.2 %reshape_reshape.12 = f32[12,32,64,12]{3,2,1,0:T(8,128)} reshape(f32[294912]{0:T(1024)S(1)} %scatter_fusion) | data formatting | bytes 2359296 | tf_op jit(solution)/shard_map/reshape;reshape | solution.py:109
  170.6 9.1 %copy.103 = f32[64,12,32,12]{0,3,2,1:T(8,128)} copy(f32[64,12,32,12]{3,0,2,1:T(8,128)} %bitcast.115) | data formatting | bytes 2359296 | tf_op jit(solution)/shard_map/transpose | solution.py:110
  187.1 12.5 %all-to-all-start.3 = ((f32[64,12,384]{2,1,0:T(8,128)}), f32[64,12,384]{2,1,0:T(8,128)}, u32[]{:S(2)}, u32[]{:S(2)}) async-start(f32[64,12,384]{2,1,0:T(8,128)} %copy.104), calls=%async_computation.3 | async-start | bytes 3145728 | tf_op jit(solution)/shard_map/all_to_all | solution.py:135
  210.1 26.2 %all-to-all-done.3 = f32[64,12,384]{2,1,0:T(8,128)} async-done(((f32[64,12,384]{2,1,0:T(8,128)}), f32[64,12,384]{2,1,0:T(8,128)}, u32[]{:S(2)}, u32[]{:S(2)}) %all-to-all-start.3) | async-done | bytes 1179680 | tf_op jit(solution)/shard_map/all_to_all | solution.py:135
  247.5 12.6 %all-to-all-done.2 = f32[4,192,384]{2,1,0:T(8,128)S(1)} async-done(((f32[4,192,384]{2,1,0:T(8,128)}), f32[4,192,384]{2,1,0:T(8,128)S(1)}, u32[]{:S(2)}, u32[]{:S(2)}) %all-to-all-start.2) | async-done | bytes 1179680 | tf_op jit(solution)/shard_map/all_to_all | solution.py:142
  299.7 15.0 %all-to-all-done.5 = f32[4,192,384]{2,1,0:T(8,128)S(1)} async-done(((f32[4,192,384]{2,1,0:T(8,128)}), f32[4,192,384]{2,1,0:T(8,128)S(1)}, u32[]{:S(2)}, u32[]{:S(2)}) %all-to-all-start.5) | async-done | bytes 1179680 | tf_op jit(solution)/shard_map/all_to_all | solution.py:146
  314.7 22.5 %fusion.14 = f32[64,12,384]{2,0,1:T(8,128)S(1)} fusion(f32[768,384,1]{1,0,2:T(8,128)S(1)} %bitcast.138, s32[64,12]{0,1:T(8,128)S(1)} %multiply_add_fusion), kind=kOutput, calls=%fused_computation.19 | convolution fusion | flops 2723807232 | bytes 2362368 | tf_op jit(solution)/shard_map/dot_general | solution.py:47
  347.3 36.5 %all-to-all-done.6 = f32[64,12,384]{2,1,0:T(8,128)} async-done(((f32[64,12,384]{2,1,0:T(8,128)}), f32[64,12,384]{2,1,0:T(8,128)}, u32[]{:S(2)}, u32[]{:S(2)}) %all-to-all-start.6) | async-done | bytes 1179680 | tf_op jit(solution)/shard_map/all_to_all | solution.py:148
  403.5 33.8 %fusion.43 = f32[12,32,768]{2,1,0:T(8,128)S(1)} fusion(f32[12,32,768]{1,2,0:T(8,128)} %reshape.345, f32[768]{0:T(1024)S(1)} %fusion.101, f32[12,32]{1,0:T(8,128)S(1)} %broadcast_add_fusion, pred[768]{0:T(1024)(128)(4,1)S(1)} %fusion.100, pred[12,32]{1,0:T(8,128)(4,1)S(1)} %broadcast_and_fusion), kind=kOutput, calls=%fused_computation.51 | convolution fusion | flops 2725871616 | bytes 2365056 | tf_op jit(solution)/shard_map/dot_general | solution.py:43
  437.3 22.5 %fusion.6 = f32[12,32,768]{1,2,0:T(8,128)} fusion(f32[12,32,768]{2,1,0:T(8,128)S(1)} %fusion.43), kind=kOutput, calls=%fused_computation.11 | convolution fusion | flops 2723807232 | bytes 2359296 | tf_op jit(solution)/shard_map/dot_general | solution.py:43
  489.0 37.3 %all-to-all-done.7 = f32[64,12,384]{2,1,0:T(8,128)} async-done(((f32[64,12,384]{2,1,0:T(8,128)}), f32[64,12,384]{2,1,0:T(8,128)}, u32[]{:S(2)}, u32[]{:S(2)}) %all-to-all-start.7) | async-done | bytes 1179680 | tf_op jit(solution)/shard_map/all_to_all | solution.py:158
  527.8 24.1 %fusion.16 = f32[4,192,384]{2,1,0:T(8,128)} fusion(f32[768,384,1]{1,0,2:T(8,128)S(1)} %reshape.381, s32[4,192]{1,0:T(4,128)S(1)} %multiply_add_fusion.1), kind=kOutput, calls=%fused_computation.21 | convolution fusion | flops 2723807232 | bytes 2362368 | tf_op jit(solution)/shard_map/dot_general | solution.py:47
  563.5 12.1 %all-to-all-done.8 = f32[4,192,384]{2,1,0:T(8,128)S(1)} async-done(((f32[4,192,384]{2,1,0:T(8,128)}), f32[4,192,384]{2,1,0:T(8,128)S(1)}, u32[]{:S(2)}, u32[]{:S(2)}) %all-to-all-start.8) | async-done | bytes 1179680 | tf_op jit(solution)/shard_map/all_to_all | solution.py:160
  620.4 12.5 %all-to-all-done.9 = f32[4,192,384]{2,1,0:T(8,128)S(1)} async-done(((f32[4,192,384]{2,1,0:T(8,128)}), f32[4,192,384]{2,1,0:T(8,128)S(1)}, u32[]{:S(2)}, u32[]{:S(2)}) %all-to-all-start.9) | async-done | bytes 1179680 | tf_op jit(solution)/shard_map/all_to_all | solution.py:164
  648.0 29.6 %all-to-all-done.13 = f32[64,12,384]{2,1,0:T(8,128)} async-done(((f32[64,12,384]{2,1,0:T(8,128)}), f32[64,12,384]{2,1,0:T(8,128)}, u32[]{:S(2)}, u32[]{:S(2)}) %all-to-all-start.13) | async-done | bytes 1179680 | tf_op jit(solution)/shard_map/all_to_all | solution.py:172
  687.5 36.0 %all-to-all-done.11 = f32[64,12,384]{2,1,0:T(8,128)} async-done(((f32[64,12,384]{2,1,0:T(8,128)}), f32[64,12,384]{2,1,0:T(8,128)}, u32[]{:S(2)}, u32[]{:S(2)}) %all-to-all-start.11) | async-done | bytes 1179680 | tf_op jit(solution)/shard_map/all_to_all | solution.py:171
  723.5 9.1 %all-to-all-start.10 = ((f32[64,12,384]{2,1,0:T(8,128)}), f32[64,12,384]{2,1,0:T(8,128)}, u32[]{:S(2)}, u32[]{:S(2)}) async-start(f32[64,12,384]{2,1,0:T(8,128)} %reshape_reshape.14), calls=%async_computation.10 | async-start | bytes 3145728 | tf_op jit(solution)/shard_map/all_to_all | solution.py:170
  799.4 25.1 %fusion.40 = f32[12,32,768]{2,1,0:T(8,128)} fusion(f32[12,32,768]{1,2,0:T(8,128)} %reshape.354, f32[767,768]{1,0:T(8,128)S(1)} %slice.35, f32[1,768]{1,0:T(1,128)S(1)} %copy-done.8, f32[12,32,768]{2,1,0:T(8,128)} %param.6, s32[12,32,768]{2,1,0:T(8,128)S(1)} %copy-done.3), kind=kOutput, calls=%fused_computation.46 | convolution fusion | flops 2719678464 | bytes 7077888 | tf_op jit(solution)/shard_map/dot_general | solution.py:43
  (126 shorter events, 348.1 us)
Async XLA Ops:
  0.7 0.6 copy-start.9
  23.4 16.6 %copy-start.7 = (f32[1,768]{1,0:T(1,128)}, f32[1,768]{1,0:T(1,128)S(1)}, u32[]{:S(2)}) copy-start(f32[1,768]{1,0:T(1,128)S(1)} %slice.39) | copy-start | bytes 9220
  23.4 16.6 %copy-start.2 = (s32[12,32,768]{2,1,0:T(8,128)S(1)}, s32[12,32,768]{2,1,0:T(8,128)}, u32[]{:S(2)}) copy-start(s32[12,32,768]{2,1,0:T(8,128)} %param.9) | copy-start | bytes 3538948
  74.4 53.9 %all-to-all-start = ((f32[64,12,384]{2,1,0:T(8,128)}), f32[64,12,384]{2,1,0:T(8,128)}, u32[]{:S(2)}, u32[]{:S(2)}) async-start(f32[64,12,384]{2,1,0:T(8,128)} %copy.97), calls=%async_computation | async-start | bytes 3145728 | tf_op jit(solution)/shard_map/all_to_all | solution.py:136
  128.3 58.8 %all-to-all-start.1 = ((f32[64,12,384]{2,1,0:T(8,128)}), f32[64,12,384]{2,1,0:T(8,128)}, u32[]{:S(2)}, u32[]{:S(2)}) async-start(f32[64,12,384]{2,1,0:T(8,128)} %copy.100), calls=%async_computation.1 | async-start | bytes 3145728 | tf_op jit(solution)/shard_map/all_to_all | solution.py:134
  187.1 49.3 %all-to-all-start.3 = ((f32[64,12,384]{2,1,0:T(8,128)}), f32[64,12,384]{2,1,0:T(8,128)}, u32[]{:S(2)}, u32[]{:S(2)}) async-start(f32[64,12,384]{2,1,0:T(8,128)} %copy.104), calls=%async_computation.3 | async-start | bytes 3145728 | tf_op jit(solution)/shard_map/all_to_all | solution.py:135
  202.0 1.5 copy-start.8
  203.5 6.6 copy-start.1
  236.4 23.7 %all-to-all-start.2 = ((f32[4,192,384]{2,1,0:T(8,128)}), f32[4,192,384]{2,1,0:T(8,128)S(1)}, u32[]{:S(2)}, u32[]{:S(2)}) async-start(f32[4,192,384]{2,1,0:T(8,128)} %bitcast.137), calls=%async_computation.2 | async-start | bytes 2359296 | tf_op jit(solution)/shard_map/all_to_all | solution.py:142
  260.1 20.3 %all-to-all-start.4 = ((f32[4,192,384]{2,1,0:T(8,128)}), f32[4,192,384]{2,1,0:T(8,128)}, u32[]{:S(2)}, u32[]{:S(2)}) async-start(f32[4,192,384]{2,1,0:T(8,128)} %reshape_reshape.13), calls=%async_computation.4 | async-start | bytes 2359296 | tf_op jit(solution)/shard_map/all_to_all | solution.py:141
  283.1 2.4 copy-start.5
  285.4 2.6 copy-start
  295.3 19.4 %all-to-all-start.5 = ((f32[4,192,384]{2,1,0:T(8,128)}), f32[4,192,384]{2,1,0:T(8,128)S(1)}, u32[]{:S(2)}, u32[]{:S(2)}) async-start(f32[4,192,384]{2,1,0:T(8,128)} %copy.111), calls=%async_computation.5 | async-start | bytes 2359296 | tf_op jit(solution)/shard_map/all_to_all | solution.py:146
  339.1 44.7 %all-to-all-start.6 = ((f32[64,12,384]{2,1,0:T(8,128)}), f32[64,12,384]{2,1,0:T(8,128)}, u32[]{:S(2)}, u32[]{:S(2)}) async-start(f32[64,12,384]{2,1,0:T(8,128)} %copy.112), calls=%async_computation.6 | async-start | bytes 3145728 | tf_op jit(solution)/shard_map/all_to_all | solution.py:148
  480.2 46.2 %all-to-all-start.7 = ((f32[64,12,384]{2,1,0:T(8,128)}), f32[64,12,384]{2,1,0:T(8,128)}, u32[]{:S(2)}, u32[]{:S(2)}) async-start(f32[64,12,384]{2,1,0:T(8,128)} %copy.118), calls=%async_computation.7 | async-start | bytes 3145728 | tf_op jit(solution)/shard_map/all_to_all | solution.py:158
  551.9 23.6 %all-to-all-start.8 = ((f32[4,192,384]{2,1,0:T(8,128)}), f32[4,192,384]{2,1,0:T(8,128)S(1)}, u32[]{:S(2)}, u32[]{:S(2)}) async-start(f32[4,192,384]{2,1,0:T(8,128)} %fusion.16), calls=%async_computation.8 | async-start | bytes 2359296 | tf_op jit(solution)/shard_map/all_to_all | solution.py:160
  579.5 2.8 copy-start.4
  579.5 2.8 copy-start.6
  593.3 20.2 %all-to-all-start.12 = ((f32[4,192,384]{2,1,0:T(8,128)}), f32[4,192,384]{2,1,0:T(8,128)}, u32[]{:S(2)}, u32[]{:S(2)}) async-start(f32[4,192,384]{2,1,0:T(8,128)} %copy.133), calls=%async_computation.12 | async-start | bytes 2359296 | tf_op jit(solution)/shard_map/all_to_all | solution.py:165
  613.5 19.4 %all-to-all-start.9 = ((f32[4,192,384]{2,1,0:T(8,128)}), f32[4,192,384]{2,1,0:T(8,128)S(1)}, u32[]{:S(2)}, u32[]{:S(2)}) async-start(f32[4,192,384]{2,1,0:T(8,128)} %copy.124), calls=%async_computation.9 | async-start | bytes 2359296 | tf_op jit(solution)/shard_map/all_to_all | solution.py:164
  632.9 44.7 %all-to-all-start.13 = ((f32[64,12,384]{2,1,0:T(8,128)}), f32[64,12,384]{2,1,0:T(8,128)}, u32[]{:S(2)}, u32[]{:S(2)}) async-start(f32[64,12,384]{2,1,0:T(8,128)} %reshape_reshape.15), calls=%async_computation.13 | async-start | bytes 3145728 | tf_op jit(solution)/shard_map/all_to_all | solution.py:172
  677.6 45.9 %all-to-all-start.11 = ((f32[64,12,384]{2,1,0:T(8,128)}), f32[64,12,384]{2,1,0:T(8,128)}, u32[]{:S(2)}, u32[]{:S(2)}) async-start(f32[64,12,384]{2,1,0:T(8,128)} %reshape.356), calls=%async_computation.11 | async-start | bytes 3145728 | tf_op jit(solution)/shard_map/all_to_all | solution.py:171
  723.5 56.1 %all-to-all-start.10 = ((f32[64,12,384]{2,1,0:T(8,128)}), f32[64,12,384]{2,1,0:T(8,128)}, u32[]{:S(2)}, u32[]{:S(2)}) async-start(f32[64,12,384]{2,1,0:T(8,128)} %reshape_reshape.14), calls=%async_computation.10 | async-start | bytes 3145728 | tf_op jit(solution)/shard_map/all_to_all | solution.py:170
  792.7 6.7 copy-start.3
where the time goes:
time: 837 us; the launch traced here: 825 us
  local copies, waits for them, and re-layouts  292 us (35%)
  waiting for transfers between devices  238 us (28%)
  matrix products  176 us (21%)
  starting transfers between devices  113 us (14%)
    dot_general x8, matrix products, along_last(): return jnp.dot(volume, matrix.T, precision=precise)  106 us
    dot_general x4, matrix products, along_first(): return jnp.tensordot(matrix, volume, axes=1, precision=precise)  59.4 us
    all_to_all x1, waiting for transfers between devices, body(): lax.all_to_all(to_north(pressure), 'row', split_axis=0, concat_axis=0, ti...  37.3 us
    all_to_all x1, waiting for transfers between devices, body(): lax.all_to_all(from_north(spectrum), 'row', split_axis=0, concat_axis=0,...  36.5 us
    all_to_all x1, waiting for transfers between devices, body(): lax.all_to_all(from_north(final_north), 'row', split_axis=0, concat_axis=...  36 us
    all_to_all x1, waiting for transfers between devices, body(): lax.all_to_all(from_north(final_upward_y), 'row', split_axis=0, concat_ax...  29.6 us
    reshape x8, local copies, waits for them, and re-layouts, to_north(): jnp.transpose(blocks, (2, 0, 1, 3))  29.2 us
    transpose x4, local copies, waits for them, and re-layouts, to_north(): jnp.transpose(blocks, (2, 0, 1, 3))  28.9 us
  transfers between devices with their start and end apart: 14, of which 12 were waited for; matrix products, arithmetic and copies ran while one was open for 21% of the time, Pallas kernels for 0%

commit v1 on v0

v1 whole, which is shorter than its diff:
```python
import functools

import jax
import jax.numpy as jnp
import numpy as np
from jax import lax
from jax.experimental import pallas as pl
from jax.experimental.pallas import tpu as pltpu
from jax.sharding import PartitionSpec as P

NX, NY, NZ = 768, 768, 128
ROWS, COLS = 64, 4
BY, BZ = NY // ROWS, NZ // COLS
F32, BF16 = jnp.float32, jnp.bfloat16


def wave(n):
    t = 2.0 * np.pi * np.arange(n) / n
    w = (14.0 / 9.0 * np.sin(t) + np.sin(2.0 * t) / 18.0) / (1.0 + 2.0 / 3.0 * np.cos(t))
    w[0] = 0.0
    w[n // 2] = 0.0
    return w


def hartley(n):
    k = np.arange(n)
    a = 2.0 * np.pi / n * (np.outer(k, k) % n)
    return np.cos(a) + np.sin(a)


def split_derivative(n, b):
    k = np.arange(n)
    first = -(np.sin(2.0 * np.pi / n * (np.outer(k, k) % n)) @ wave(n)) / n
    d = -first
    d = -d
    r = (np.sqrt(5.0) - 3.0) / 2.0
    dense = d[(k[:, None] - k[None, :]) % n]
    blocks = n // b
    local = dense[:b, :b]
    c0 = d[2] * (1.0 - r**n) / (r**2 - r ** (n - 2))
    c0 = c0 / (1.0 - r**n)
    extra = d[1] - c0 * (r - r ** (n - 1))
    j = np.arange(b)
    moments = np.zeros((4, b))
    moments[0] = r ** (b - 1 - j)
    moments[1] = r**j
    moments[2, b - 1] = 1.0
    moments[3, 0] = 1.0
    far = np.zeros((n, blocks, 4))
    i = np.arange(b)
    for big_i in range(blocks):
        for big_j in range(blocks):
            if big_i == big_j:
                continue
            gap = (big_i - big_j) % blocks
            rows = slice(big_i * b, (big_i + 1) * b)
            far[rows, big_j, 0] = c0 * r ** (b * gap + i - (b - 1)).astype(np.float64)
            far[rows, big_j, 1] = -c0 * r ** (n - b * gap - i).astype(np.float64)
            if gap == 1:
                far[big_i * b, big_j, 2] = extra
            if gap == blocks - 1:
                far[big_i * b + b - 1, big_j, 3] = -extra
    return dense, local, moments, far


def halves(a):
    a = np.asarray(a, np.float32)
    hi = a.astype(jnp.bfloat16)
    lo = (a - hi.astype(np.float32)).astype(jnp.bfloat16)
    return hi, lo


@functools.lru_cache(maxsize=None)
def constants():
    dense_x = split_derivative(NX, BY)[0]
    _, loc_y, mom_y, far_y = split_derivative(NY, BY)
    _, loc_z, mom_z, far_z = split_derivative(NZ, BZ)
    hx, hy, hz = hartley(NX), hartley(NY), hartley(NZ)
    eye_y, eye_z = np.eye(BY), np.eye(BZ)
    lv_q, lv_m = np.kron(loc_y, eye_z), np.kron(mom_y, eye_z)
    lw_q, lw_m = np.kron(eye_y, loc_z), np.kron(eye_y, mom_z)
    parts = []
    for h in range(2):
        parts.append(np.concatenate([lv_q[h * 192:(h + 1) * 192], lw_q[h * 192:(h + 1) * 192]], 1))
        vm = lv_m[h * 64:(h + 1) * 64]
        parts.append(np.concatenate([vm, np.zeros_like(vm)], 1))
        wm = lw_m[h * 24:(h + 1) * 24]
        parts.append(np.concatenate([np.zeros_like(wm), wm], 1))
    left = np.concatenate(parts, 0)
    far_hz = np.einsum("kz,zcm->kcm", hz, far_z)
    wz = np.zeros((6, NZ, 224))
    for y in range(6):
        wz[y, :, :NZ] = hz
        wide = np.zeros((NZ, COLS, 6, 4))
        wide[:, :, y, :] = far_hz
        wz[y, :, NZ:] = wide.reshape(NZ, 96)
    far_hy = np.einsum("ky,yjm->kjm", hy, far_y)
    wy = np.concatenate([hy.reshape(NY, ROWS, BY), far_hy], 2).reshape(NY, ROWS * 16)
    out = {}
    for name, value in (
        ("hx", hx),
        ("fwd_dx", dense_x.T @ hx),
        ("bwd_dx", hx @ dense_x.T),
        ("left", left),
        ("left_t", left.T),
        ("wz", wz),
        ("wz_t", np.swapaxes(wz, 1, 2)),
        ("wy", wy),
        ("wy_t", wy.T),
    ):
        out[name] = halves(value)
    out["wave2"] = tuple(np.asarray(wave(n) ** 2, np.float32) for n in (NX, NY, NZ))
    return out


def two(a):
    hi = a.astype(BF16)
    return hi, (a - hi.astype(F32)).astype(BF16)


def dot(a, b):
    return jnp.dot(a, b, preferred_element_type=F32)


def dot3(a, b):
    return dot(a[0], b[0]) + (dot(a[0], b[1]) + dot(a[1], b[0]))


def low_half(shape):
    return lax.broadcasted_iota(jnp.int32, shape, len(shape) - 1) < 64


def join(first, second):
    return jnp.where(low_half(first.shape), first, pltpu.roll(second, 64, 1))


def join_high(first, second):
    return jnp.where(low_half(first.shape), pltpu.roll(first, 64, 1), second)


def set_inflow(place, cells, speed, upward):
    def step(t, carry):
        y = t // 2
        row = place[0] * BY + y
        k = (16 * row + 4 * place[1]) // 3 + t % 2
        rel = cells[k] - (row * NZ + place[1] * BZ) * NX
        inside = (rel >= 0) & (rel < BZ * NX)
        rel = jnp.where(inside, rel, 0)
        line = rel // NX
        x = jnp.where(inside, rel - line * NX, -1)
        at = pl.ds(y * BZ + line, 1)
        lanes = lax.broadcasted_iota(jnp.int32, (1, NX), 1)
        upward[at, :] = jnp.where(lanes == x, speed[k], upward[at, :])
        return carry

    lax.fori_loop(0, 2 * BY, step, 0)


def forward_x(place, cells, speed, u, v, w, solid, lh, ll, hh, hl, dh, dl, out, upward, sh, sl):
    fluid = (1 - solid[...]).astype(F32)
    upward[...] = w[...] * fluid
    set_inflow(place, cells, speed, upward)
    u2 = two(u[...] * fluid)
    left = (lh[...], ll[...])
    for n in range(3):
        at = slice(n * 256, (n + 1) * 256)
        both = jnp.concatenate([v[:, at] * fluid[:, at], upward[:, at]], 0)
        s = dot3(left, two(both))
        hi, lo = two(s)
        sh[:, at] = hi
        sl[:, at] = lo
    s2 = (sh[...], sl[...])
    for n in range(3):
        at = slice(n * 256, (n + 1) * 256)
        r = dot3(s2, (hh[:, at], hl[:, at]))
        d = dot3(u2, (dh[:, at], dl[:, at]))
        top = jnp.concatenate([r[:192] + d[:192], r[192:280]], 0)
        bottom = jnp.concatenate([r[280:472] + d[192:], r[472:]], 0)
        for t in range(2):
            a, b = top[:, t * 128:(t + 1) * 128], bottom[:, t * 128:(t + 1) * 128]
            c = 2 * n + t
            if c < 4:
                out[c, :, 0:128] = a
                out[c, :, 128:256] = b
            else:
                c = 2 * (c - 4)
                out[c, :, 256:384] = join(a, b)
                out[c + 1, :, 256:384] = join_high(a, b)


def backward_x(place, cells, speed, u, v, w, solid, x, lh, ll, hh, hl, dh, dl, uo, vo, wo, upward, th, tl, ph, plo):
    fluid = (1 - solid[...]).astype(F32)
    upward[...] = w[...] * fluid
    set_inflow(place, cells, speed, upward)
    for t in range(6):
        if t < 4:
            a, b = x[t, :, 0:128], x[t, :, 128:256]
        else:
            c = 2 * (t - 4)
            e, o = x[c, :, 256:384], x[c + 1, :, 256:384]
            a, b = join(e, o), join_high(e, o)
        hi, lo = two(jnp.concatenate([a, b], 0))
        th[:, t * 128:(t + 1) * 128] = hi
        tl[:, t * 128:(t + 1) * 128] = lo
    t2 = (th[...], tl[...])
    left = (lh[...], ll[...])
    for n in range(3):
        at = slice(n * 256, (n + 1) * 256)
        p = dot3(t2, (hh[:, at], hl[:, at]))
        d = dot3(t2, (dh[:, at], dl[:, at]))
        uo[0:192, at] = u[0:192, at] * fluid[0:192, at] - d[0:192]
        uo[192:384, at] = u[192:384, at] * fluid[192:384, at] - d[280:472]
        g = dot3(left, two(p))
        vo[:, at] = v[:, at] * fluid[:, at] + g[0:384]
        wo[:, at] = upward[:, at] + g[384:768]


def forward_z(x, wh, wl, out):
    marks = [x[c, 256:280, :] for c in range(COLS)]
    for y in range(8):
        own = [x[c, y * 32:(y + 1) * 32, :] for c in range(COLS)]
        if y < 6:
            z = dot3((wh[y], wl[y]), two(jnp.concatenate(own + marks, 0)))
            planes = (y, 6 + y)
        else:
            z = dot3((wh[0, :, 0:128], wl[0, :, 0:128]), two(jnp.concatenate(own, 0)))
            planes = (6 + y, 8 + y)
        a, b = z[0:64], z[64:128]
        for half, plane in enumerate(planes):
            tile = slice(half * 128, (half + 1) * 128)
            pick = join_high if half else join
            third = pick(a[:, 256:384], b[:, 256:384])
            for k, value in enumerate((a[:, tile], b[:, tile], third)):
                out[pl.ds(16 * k + plane, 64, stride=48), :] = value


def backward_z(x, wh, wl, out):
    total = None
    for y in range(8):
        planes = (y, 6 + y) if y < 6 else (6 + y, 8 + y)
        t = [[x[pl.ds(16 * k + p, 64, stride=48), :] for k in range(3)] for p in planes]
        low = jnp.concatenate([t[0][0], t[1][0], join(t[0][2], t[1][2])], 1)
        high = jnp.concatenate([t[0][1], t[1][1], join_high(t[0][2], t[1][2])], 1)
        z = two(jnp.concatenate([low, high], 0))
        if y < 6:
            r = dot3((wh[y], wl[y]), z)
            total = r[128:224] if total is None else total + r[128:224]
        else:
            r = dot3((wh[0, 0:128, :], wl[0, 0:128, :]), z)
        for c in range(COLS):
            out[c, y * 32:(y + 1) * 32, :] = r[c * 32:(c + 1) * 32]
    for c in range(COLS):
        out[c, 256:280, :] = total[c * 24:(c + 1) * 24]


def solve_y(x, kappa2, wave2, ah, al, bh, bl, out):
    tiles = [x[:, 16 * t:16 * (t + 1), :].reshape(ROWS * 16, 128) for t in range(3)]
    s = dot3((ah[...], al[...]), two(jnp.concatenate(tiles, 1)))
    den = wave2[...] + kappa2[...]
    null = den == 0.0
    s = jnp.where(null, 0.0, -s / (jnp.where(null, 1.0, den) * float(NX * NY * NZ)))
    r = dot3((bh[...], bl[...]), two(s))
    for t in range(3):
        out[:, 16 * t:16 * (t + 1), :] = r[:, 128 * t:128 * (t + 1)].reshape(ROWS, 16, 128)


def call(kernel, out_shape, args, scratch=(), scalars=0, flops=10**9):
    spec_v = pl.BlockSpec(memory_space=pltpu.VMEM)
    spec_s = pl.BlockSpec(memory_space=pltpu.SMEM)
    many = isinstance(out_shape, (tuple, list))
    return pl.pallas_call(
        kernel,
        out_shape=out_shape,
        in_specs=[spec_s] * scalars + [spec_v] * (len(args) - scalars),
        out_specs=[spec_v] * len(out_shape) if many else spec_v,
        scratch_shapes=list(scratch),
        compiler_params=pltpu.CompilerParams(vmem_limit_bytes=48 * 2**20),
        name=kernel.__name__,
    )(*args)


def body(east_flow, north_flow, upward_flow, solid, inflow_cells, inflow_speed):
    k = constants()
    row, col = lax.axis_index("row"), lax.axis_index("col")
    place = jnp.stack([row, col]).astype(jnp.int32)
    flat = (BY * BZ, NX)
    fields = [a.reshape(flat) for a in (east_flow, north_flow, upward_flow, solid)]
    sds = jax.ShapeDtypeStruct
    mov = (COLS, 280, 384)
    x = call(
        forward_x, sds(mov, F32),
        [place, inflow_cells, inflow_speed, *fields, *k["left"], *k["hx"], *k["fwd_dx"]],
        [pltpu.VMEM(flat, F32), pltpu.VMEM((560, NX), BF16), pltpu.VMEM((560, NX), BF16)], 3,
    )
    x = lax.all_to_all(x, "col", 0, 0, tiled=True)
    x = call(forward_z, sds((ROWS * 48, 128), F32), [x, *k["wz"]])
    x = lax.all_to_all(x.reshape(ROWS, 48, 128), "row", 0, 0, tiled=True)
    wx2, wy2, wz2 = [jnp.asarray(a) for a in k["wave2"]]
    x128 = lax.dynamic_slice_in_dim(wx2, 128 * col, 128)
    x64 = lax.dynamic_slice_in_dim(wx2, 512 + 64 * col, 64)
    z0 = lax.dynamic_slice_in_dim(wz2, row, 1)
    z1 = lax.dynamic_slice_in_dim(wz2, 64 + row, 1)
    kappa2 = jnp.concatenate([x128 + z0, x128 + z1, x64 + z0, x64 + z1]).reshape(1, 384)
    x = call(solve_y, sds((ROWS, 48, 128), F32), [x, kappa2, wy2.reshape(NY, 1), *k["wy"], *k["wy_t"]])
    x = lax.all_to_all(x, "row", 0, 0, tiled=True).reshape(ROWS * 48, 128)
    x = call(backward_z, sds(mov, F32), [x, *k["wz_t"]])
    x = lax.all_to_all(x, "col", 0, 0, tiled=True)
    outs = call(
        backward_x, [sds(flat, F32)] * 3,
        [place, inflow_cells, inflow_speed, *fields, x, *k["left_t"], *k["hx"], *k["bwd_dx"]],
        [pltpu.VMEM(flat, F32), pltpu.VMEM((560, NX), BF16), pltpu.VMEM((560, NX), BF16),
         pltpu.VMEM((8, 128), F32), pltpu.VMEM((8, 128), F32)], 3,
    )
    return tuple(o.reshape(BY, BZ, NX) for o in outs)


def solution(mesh):
    spec = P("row", "col", None)
    return jax.shard_map(
        body, mesh=mesh, in_specs=(spec,) * 4 + (P(), P()), out_specs=(spec,) * 3, check_vma=False
    )
```

time: 837 us -> 201 us (0.24); the launches traced: 825 us -> 200 us
  local copies, waits for them, and re-layouts: 292 us -> 8.23 us
  waiting for transfers between devices: 238 us -> 33.8 us
  matrix products: 176 us -> 0 us
  blocking collectives: 0 us -> 103 us
  starting transfers between devices: 113 us -> 12.7 us
  Pallas kernels: 0 us -> 37.3 us
    all_to_all x14 -> x1, waiting for transfers between devices: 238 us -> 33.8 us  [body(): x = lax.all_to_all(x.reshape(ROWS, 48, 128), 'row', 0, 0, tiled=True)]
    dot_general x14 -> x0, matrix products: 176 us -> none  [the longest x8 106 us: along_last(): return jnp.dot(volume, matrix.T, precision=precise)]
    reshape x29 -> x1, local copies, waits for them, and re-layouts: 111 us -> 0.01 us  [body(): jnp.concatenate([x128 + z0, x128 + z1, x64 + z0, x64 + z1]).reshape(1, 384)]
    all_to_all x0 -> x3, blocking collectives: none -> 103 us  [the longest x2 57.7 us: body(): x = lax.all_to_all(x, 'col', 0, 0, tiled=True)]
    all_to_all x14 -> x1, starting transfers between devices: 113 us -> 12.7 us  [body(): x = lax.all_to_all(x.reshape(ROWS, 48, 128), 'row', 0, 0, tiled=True)]
    transpose x14 -> x0, local copies, waits for them, and re-layouts: 71.9 us -> none  [the longest x4 28.9 us: to_north(): jnp.transpose(blocks, (2, 0, 1, 3))]
    pallas_call x0 -> x5, Pallas kernels: none -> 37.3 us  [call(): pl.pallas_call(kernel, out_shape=out_shape, in_specs=[spec_s] * scalars +...]
    another operation x8 -> x0, local copies, waits for them, and re-layouts: 31.6 us -> none  [the longest x1 15.2 us: to_north(): blocks = volume.reshape(north_local, upward_local, row_count, east_local)]
  transfers between devices with their start and end apart: 14 -> 1, of which waited for: 12 -> 1; matrix products, arithmetic and copies ran while one was open for 21% -> 2% of each run, Pallas kernels for 0% -> 0%
where the time goes in v1:
time: 201 us; the launch traced here: 200 us
  blocking collectives  103 us (51%)
  Pallas kernels  37.3 us (19%)
  waiting for transfers between devices  33.8 us (17%)
  starting transfers between devices  12.7 us (6%)
  local copies, waits for them, and re-layouts  8.23 us (4%)
  other arithmetic  4.26 us (2%)
    all_to_all x2, blocking collectives, body(): x = lax.all_to_all(x, 'col', 0, 0, tiled=True)  57.7 us
    all_to_all x1, blocking collectives, body(): x = lax.all_to_all(x, 'row', 0, 0, tiled=True).reshape(ROWS * 48, 128)  45.6 us
    pallas_call x5, Pallas kernels, call(): pl.pallas_call(kernel, out_shape=out_shape, in_specs=[spec_s] * scalars +...  37.3 us
    all_to_all x1, waiting for transfers between devices, body(): x = lax.all_to_all(x.reshape(ROWS, 48, 128), 'row', 0, 0, tiled=True)  33.8 us
    all_to_all x1, starting transfers between devices, body(): x = lax.all_to_all(x.reshape(ROWS, 48, 128), 'row', 0, 0, tiled=True)  12.7 us
    unnamed x42, local copies, waits for them, and re-layouts  7.63 us
  transfers between devices with their start and end apart: 1, of which 1 were waited for; matrix products, arithmetic and copies ran while one was open for 2% of the time, Pallas kernels for 0%

profile of v1, /device:TPU:1, one launch (start us, length us, event | category | flops | bytes accessed | tf_op | source)
XLA Modules:
  0.0 200.4 jit_solution(1332071185477753990)
XLA Ops:
  0.6 0.1 pad_add_fusion.place
  0.7 1.3 copy-done
  2.0 1.3 copy-done.2
  3.3 1.3 copy-done.4
  4.5 1.2 copy-done.9
  5.7 1.2 copy-done.10
  6.8 0.7 copy-done.16
  7.6 0.7 copy-done.18
  8.3 12.8 %forward_x.1 = f32[4,280,384]{2,1,0:T(8,128)} custom-call(s32[2]{0:T(128)S(1)} %pad_add_fusion.place, s32[4096]{0:T(1024)S(1)} %copy-done.16, f32[4096]{0:T(1024)S(1)} %copy-done.18, f32[384,768]{1,0:T(8,128)S(1)} %bitcast.14, f32[384,768]{1,0:T(8,128)S(1)} %bitcast.16, f32[384,768]{1,0:T(8,128)S(1)} %bitcast.18, s32[384,768]{1,0:T(8,128)} %bitcast.20, ...), custom_call_target="tpu_custom_call" | custom-call | tf_op jit(solution)/shard_map/forward_x/pallas_call | solution.py:271
  21.1 28.1 %all_to_all.20.x = f32[4,280,384]{2,1,0:T(8,128)S(1)} all-to-all(f32[4,280,384]{2,1,0:T(8,128)} %forward_x.1), channel_id=1, replica_groups=mesh['row'=64,'col'=4] {'col'}, dimensions={0} | all-to-all | bytes 3440640 | tf_op jit(solution)/shard_map/all_to_all | solution.py:295
  49.2 2.6 %forward_z.1 = f32[3072,128]{1,0:T(8,128)} custom-call(f32[4,280,384]{2,1,0:T(8,128)S(1)} %all_to_all.20.x, bf16[6,128,224]{2,1,0:T(8,128)(2,1)S(1)} %copy-done.13, bf16[6,128,224]{2,1,0:T(8,128)(2,1)S(1)} %copy-done.12), custom_call_target="tpu_custom_call" | custom-call | tf_op jit(solution)/shard_map/forward_z/pallas_call | solution.py:271
  51.8 12.7 %all-to-all-start.1 = ((f32[64,48,128]{2,1,0:T(8,128)}), f32[64,48,128]{2,1,0:T(8,128)S(1)}, u32[]{:S(2)}, u32[]{:S(2)}) async-start(f32[64,48,128]{2,1,0:T(8,128)} %bitcast.6), calls=%async_computation.1 | async-start | bytes 3145728 | tf_op jit(solution)/shard_map/all_to_all | solution.py:297
  64.5 0.6 fusion
  65.1 2.1 %dynamic-slice_add_fusion.1 = (f32[64]{0:T(128)S(1)}, f32[64]{0:T(128)S(1)}) fusion(f32[768]{0:T(1024)} %constant.71.clone, s32[]{:T(128)S(6)} %select_n.15, f32[]{:T(128)} %bitcast.7, f32[]{:T(128)} %bitcast.8), kind=kLoop, calls=%fused_computation.3 | loop fusion | flops 128 | bytes 780 | tf_op jit(solution)/shard_map/add | solution.py:303
  67.1 2.1 %dynamic-slice_add_fusion.3 = (f32[128]{0:T(128)S(1)}, f32[128]{0:T(128)S(1)}) fusion(f32[768]{0:T(1024)} %constant.71.clone, s32[]{:T(128)S(6)} %select_n.12, f32[]{:T(128)} %bitcast.7, f32[]{:T(128)} %bitcast.8), kind=kLoop, calls=%fused_computation.5 | loop fusion | flops 256 | bytes 1548 | tf_op jit(solution)/shard_map/add | solution.py:303
  69.2 0.1 pad_maximum_fusion
  69.3 33.8 %all-to-all-done.1.x = f32[64,48,128]{2,1,0:T(8,128)S(1)} async-done(((f32[64,48,128]{2,1,0:T(8,128)}), f32[64,48,128]{2,1,0:T(8,128)S(1)}, u32[]{:S(2)}, u32[]{:S(2)}) %all-to-all-start.1) | async-done | bytes 1572896 | tf_op jit(solution)/shard_map/all_to_all | solution.py:297
  103.0 7.6 %solve_y.1 = f32[64,48,128]{2,1,0:T(8,128)S(1)} custom-call(f32[64,48,128]{2,1,0:T(8,128)S(1)} %all-to-all-done.1.x, f32[1,384]{1,0:T(1,128)S(1)} %reshape.44.kappa2, f32[768,1]{1,0:T(8,128)S(1)} %copy-done.11, bf16[768,1024]{1,0:T(8,128)(2,1)S(1)} %copy-done.6, bf16[768,1024]{1,0:T(8,128)(2,1)} %constant.74.clone.al, bf16[1024,768]{1,0:T(8,128)(2,1)} %constant.75.clone.bh, ...), custom_call_target="tpu_custom_call" | custom-call | tf_op jit(solution)/shard_map/solve_y/pallas_call | solution.py:271
  110.7 0.0 copy-start.14
  110.7 0.0 copy-start.15
  110.7 45.6 %all_to_all.21 = f32[64,48,128]{2,1,0:T(8,128)S(1)} all-to-all(f32[64,48,128]{2,1,0:T(8,128)S(1)} %solve_y.1), channel_id=1, replica_groups=mesh['row'=64,'col'=4] {'row'}, dimensions={0} | all-to-all | bytes 3145728 | tf_op jit(solution)/shard_map/all_to_all | solution.py:305
  156.3 1.3 backward_z.1
  157.7 29.6 %all_to_all.22.x = f32[4,280,384]{2,1,0:T(8,128)} all-to-all(f32[4,280,384]{2,1,0:T(8,128)S(1)} %backward_z.1), channel_id=1, replica_groups=mesh['row'=64,'col'=4] {'col'}, dimensions={0} | all-to-all | bytes 3440640 | tf_op jit(solution)/shard_map/all_to_all | solution.py:307
  187.4 13.0 %backward_x.1 = (f32[384,768]{1,0:T(8,128)}, f32[384,768]{1,0:T(8,128)}, f32[384,768]{1,0:T(8,128)}) custom-call(s32[2]{0:T(128)S(1)} %pad_add_fusion.place, s32[4096]{0:T(1024)S(1)} %copy-done.17, f32[4096]{0:T(1024)S(1)} %copy-done.19, f32[384,768]{1,0:T(8,128)S(1)} %bitcast.15, f32[384,768]{1,0:T(8,128)S(1)} %bitcast.17, f32[384,768]{1,0:T(8,128)S(1)} %bitcast.19, ...), custom_call_target="tpu_custom_call" | custom-call | tf_op jit(solution)/shard_map/backward_x/pallas_call | solution.py:271
  (34 shorter events, 0.1 us)
Async XLA Ops:
  0.7 1.3 copy-start
  2.0 1.3 copy-start.2
  3.3 1.3 copy-start.4
  4.5 1.2 copy-start.9
  5.7 1.2 copy-start.10
  6.8 0.7 copy-start.16
  7.6 0.7 copy-start.18
  21.1 28.1 %copy-start.12 = (bf16[6,128,224]{2,1,0:T(8,128)(2,1)S(1)}, bf16[6,128,224]{2,1,0:T(8,128)(2,1)}, u32[]{:S(2)}) copy-start(bf16[6,128,224]{2,1,0:T(8,128)(2,1)} %constant.70.clone.wl) | copy-start | bytes 1032196
  21.1 28.1 %copy-start.13 = (bf16[6,128,224]{2,1,0:T(8,128)(2,1)S(1)}, bf16[6,128,224]{2,1,0:T(8,128)(2,1)}, u32[]{:S(2)}) copy-start(bf16[6,128,224]{2,1,0:T(8,128)(2,1)} %constant.69.clone.wh) | copy-start | bytes 1032196
  51.8 12.7 %copy-start.20 = (f32[128]{0:T(128)S(1)}, f32[128]{0:T(128)}, u32[]{:S(2)}) copy-start(f32[128]{0:T(128)} %constant.72.clone) | copy-start | bytes 1540
  51.8 51.3 %copy-start.6 = (bf16[768,1024]{1,0:T(8,128)(2,1)S(1)}, bf16[768,1024]{1,0:T(8,128)(2,1)}, u32[]{:S(2)}) copy-start(bf16[768,1024]{1,0:T(8,128)(2,1)} %constant.73.clone.ah) | copy-start | bytes 4718596
  51.8 51.3 %copy-start.11 = (f32[768,1]{1,0:T(8,128)S(1)}, f32[768,1]{1,0:T(8,128)}, u32[]{:S(2)}) copy-start(f32[768,1]{1,0:T(8,128)} %constant.87.wave2) | copy-start | bytes 9220
  51.8 51.3 %all-to-all-start.1 = ((f32[64,48,128]{2,1,0:T(8,128)}), f32[64,48,128]{2,1,0:T(8,128)S(1)}, u32[]{:S(2)}, u32[]{:S(2)}) async-start(f32[64,48,128]{2,1,0:T(8,128)} %bitcast.6), calls=%async_computation.1 | async-start | bytes 3145728 | tf_op jit(solution)/shard_map/all_to_all | solution.py:297
  110.7 45.6 %copy-start.14 = (bf16[6,224,128]{2,1,0:T(8,128)(2,1)S(1)}, bf16[6,224,128]{2,1,0:T(8,128)(2,1)}, u32[]{:S(2)}) copy-start(bf16[6,224,128]{2,1,0:T(8,128)(2,1)} %constant.78.clone.wl) | copy-start | bytes 1032196
  110.7 45.6 %copy-start.15 = (bf16[6,224,128]{2,1,0:T(8,128)(2,1)S(1)}, bf16[6,224,128]{2,1,0:T(8,128)(2,1)}, u32[]{:S(2)}) copy-start(bf16[6,224,128]{2,1,0:T(8,128)(2,1)} %constant.77.clone.wh) | copy-start | bytes 1032196
  156.3 31.0 %copy-start.5 = (f32[12,32,768]{2,1,0:T(8,128)S(1)}, f32[12,32,768]{2,1,0:T(8,128)}, u32[]{:S(2)}) copy-start(f32[12,32,768]{2,1,0:T(8,128)} %param.29) | copy-start | bytes 3538948
  156.3 31.0 %copy-start.8 = (bf16[768,560]{1,0:T(8,128)(2,1)S(1)}, bf16[768,560]{1,0:T(8,128)(2,1)}, u32[]{:S(2)}) copy-start(bf16[768,560]{1,0:T(8,128)(2,1)} %constant.79.clone.lh) | copy-start | bytes 2580484
  157.6 29.7 %copy-start.1 = (f32[12,32,768]{2,1,0:T(8,128)S(1)}, f32[12,32,768]{2,1,0:T(8,128)}, u32[]{:S(2)}) copy-start(f32[12,32,768]{2,1,0:T(8,128)} %param.27) | copy-start | bytes 3538948
  157.6 29.7 %copy-start.3 = (f32[12,32,768]{2,1,0:T(8,128)S(1)}, f32[12,32,768]{2,1,0:T(8,128)}, u32[]{:S(2)}) copy-start(f32[12,32,768]{2,1,0:T(8,128)} %param.28) | copy-start | bytes 3538948
  157.6 29.7 %copy-start.7 = (bf16[768,560]{1,0:T(8,128)(2,1)S(1)}, bf16[768,560]{1,0:T(8,128)(2,1)}, u32[]{:S(2)}) copy-start(bf16[768,560]{1,0:T(8,128)(2,1)} %constant.80.clone.ll) | copy-start | bytes 2580484
  157.6 29.7 %copy-start.17 = (s32[4096]{0:T(1024)S(1)}, s32[4096]{0:T(1024)}, u32[]{:S(2)}) copy-start(s32[4096]{0:T(1024)} %cells.3) | copy-start | bytes 49156
  157.7 29.7 %copy-start.19 = (f32[4096]{0:T(1024)S(1)}, f32[4096]{0:T(1024)}, u32[]{:S(2)}) copy-start(f32[4096]{0:T(1024)} %speed.3) | copy-start | bytes 49156

commit v2 on v1

--- a/solution.py
+++ b/solution.py
@@ -70,6 +70,56 @@
     return hi, lo
 
 
+RATIO = (np.sqrt(5.0) - 3.0) / 2.0
+TAIL, EDGE = 25.0 / 12.0, -1.0 / 12.0
+
+
+def mode_tables():
+    wx, wz = wave(NX), wave(NZ)
+    kappa = np.sqrt(wz[:, None] ** 2 + wx[None, :] ** 2).reshape(-1)
+    null = kappa == 0.0
+    kap = np.where(null, 1.0, kappa)
+    c = np.stack([np.full_like(kap, 1 / 36), kap / 3 + 7 / 9, kap, kap / 3 - 7 / 9, np.full_like(kap, -1 / 36)], 1)
+    companion = np.zeros((kap.size, 4, 4))
+    companion[:, 0, :] = -c[:, 1:] / c[:, :1]
+    companion[:, 1, 0] = companion[:, 2, 1] = companion[:, 3, 2] = 1.0
+    z = np.sort(np.linalg.eigvals(companion).real, 1)
+    c = c[:, :, None]
+    for _ in range(3):
+        value = (((c[:, 0] * z + c[:, 1]) * z + c[:, 2]) * z + c[:, 3]) * z + c[:, 4]
+        slope = ((4 * c[:, 0] * z + 3 * c[:, 1]) * z + 2 * c[:, 2]) * z + c[:, 3]
+        z = z - value / slope
+    z = np.stack([z[:, 3], 1 / z[:, 1], z[:, 2], 1 / z[:, 0]], 1)
+    cos = (z + 1 / z) / 2
+    lead = 14 / 9 + cos / 9
+    slope = -2 * cos * lead**2 + (1 - cos**2) * 2 * lead / 9 + kap[:, None] ** 2 * 2 * (1 + 2 * cos / 3) * 2 / 3
+    a = -((1 + 2 * cos / 3) ** 2) / slope * 2 * z / (1 - z * z)
+    a = np.where(null[:, None], 0.0, a) / float(NX * NZ)
+    turn = np.where(null[:, None], 1.0, z**BY)
+    close = np.where(null[:, None], 1.0, 1 / (1 - z**NY))
+    z = np.where(null[:, None], 0.5, z)
+
+    def place(t):
+        t = t.reshape(2, ROWS, NX, -1)
+        out = np.zeros((COLS, ROWS, 3, 128, t.shape[-1]))
+        for c in range(COLS):
+            low, high = t[:, :, 128 * c:128 * c + 128], t[:, :, 512 + 64 * c:576 + 64 * c]
+            out[c, :, 0], out[c, :, 1] = low[0], low[1]
+            out[c, :, 2, :64], out[c, :, 2, 64:] = high[0], high[1]
+        return out
+
+    local = place(np.concatenate([z, a], 1)).transpose(0, 4, 2, 1, 3)
+    cycle = place(np.concatenate([turn, turn, close, close], 1))
+    cycle = cycle.transpose(0, 1, 2, 4, 3).reshape(COLS, ROWS, 3, 2, 8, 128).transpose(0, 1, 3, 2, 4, 5)
+    return local.astype(np.float32), np.ascontiguousarray(cycle.reshape(COLS, ROWS, 2, 24, 128)).astype(np.float32)
+
+
+@functools.lru_cache(maxsize=None)
+def null_inverse():
+    _, local, moments, _ = split_derivative(NY, BY)
+    return np.linalg.pinv(np.concatenate([local, moments], 0))
+
+
 @functools.lru_cache(maxsize=None)
 def constants():
     dense_x = split_derivative(NX, BY)[0]
@@ -94,8 +144,6 @@
         wide = np.zeros((NZ, COLS, 6, 4))
         wide[:, :, y, :] = far_hz
         wz[y, :, NZ:] = wide.reshape(NZ, 96)
-    far_hy = np.einsum("ky,yjm->kjm", hy, far_y)
-    wy = np.concatenate([hy.reshape(NY, ROWS, BY), far_hy], 2).reshape(NY, ROWS * 16)
     out = {}
     for name, value in (
         ("hx", hx),
@@ -105,11 +153,9 @@
         ("left_t", left.T),
         ("wz", wz),
         ("wz_t", np.swapaxes(wz, 1, 2)),
-        ("wy", wy),
-        ("wy_t", wy.T),
     ):
         out[name] = halves(value)
-    out["wave2"] = tuple(np.asarray(wave(n) ** 2, np.float32) for n in (NX, NY, NZ))
+    out["local"], out["cycle"] = mode_tables()
     return out
 
 
@@ -188,7 +234,7 @@
                 out[c + 1, :, 256:384] = join_high(a, b)
 
 
-def backward_x(place, cells, speed, u, v, w, solid, x, lh, ll, hh, hl, dh, dl, uo, vo, wo, upward, th, tl, ph, plo):
+def backward_x(place, cells, speed, u, v, w, solid, x, lh, ll, hh, hl, dh, dl, uo, vo, wo, upward, th, tl):
     fluid = (1 - solid[...]).astype(F32)
     upward[...] = w[...] * fluid
     set_inflow(place, cells, speed, upward)
@@ -215,7 +261,9 @@
         wo[:, at] = upward[:, at] + g[384:768]
 
 
-def forward_z(x, wh, wl, out):
+def forward_z(place, x, wh, wl, table, out, keep, sem):
+    copy = pltpu.make_async_copy(table.at[place[1]], keep.at[pl.ds(16, 8)], sem)
+    copy.start()
     marks = [x[c, 256:280, :] for c in range(COLS)]
     for y in range(8):
         own = [x[c, y * 32:(y + 1) * 32, :] for c in range(COLS)]
@@ -229,16 +277,136 @@
         for half, plane in enumerate(planes):
             tile = slice(half * 128, (half + 1) * 128)
             pick = join_high if half else join
-            third = pick(a[:, 256:384], b[:, 256:384])
-            for k, value in enumerate((a[:, tile], b[:, tile], third)):
-                out[pl.ds(16 * k + plane, 64, stride=48), :] = value
-
-
-def backward_z(x, wh, wl, out):
+            keep[plane, 0] = a[:, tile]
+            keep[plane, 1] = b[:, tile]
+            keep[plane, 2] = pick(a[:, 256:384], b[:, 256:384])
+    copy.wait()
+
+    def step(j, carry):
+        for t in range(3):
+            at = lambda p: keep[p, t, pl.ds(8 * j, 8), :]
+            q = [at(p) for p in range(BY)]
+            plus, minus, last, first = [at(BY + p) for p in range(4)]
+            for k in range(4):
+                z = at(16 + k)
+                near, far = tails(z)
+                right = -z * (near * minus + EDGE * first)
+                left = z * (near * plus + EDGE * last)
+                for i in range(BY):
+                    right = z * (right + q[i])
+                    left = z * (left + q[BY - 1 - i])
+                right = right + (z * far * plus + EDGE * last)
+                left = left - (z * far * minus + EDGE * first)
+                out[pl.ds(192 * j + 8 * t + k, 8, stride=24), :] = right
+                out[pl.ds(192 * j + 8 * t + 4 + k, 8, stride=24), :] = left
+        return carry
+
+    lax.fori_loop(0, ROWS // 8, step, 0)
+    for t in range(2):
+        null = keep[20, t, 0:8, :] == 0.0
+        sums = null_sums([keep[p, t, 0:8, :] for p in range(16)])
+        for k in range(2):
+            for m in (k, 4 + k):
+                at = pl.ds(8 * t + m, 8, stride=24)
+                out[at, :] = jnp.where(null, sums[k], out[at, :])
+
+
+def weigh(weights, values):
+    return sum(float(w) * value for w, value in zip(weights, values))
+
+
+def null_sums(planes):
+    inverse = null_inverse()
+    return weigh(inverse.sum(0), planes), weigh(((-1.0) ** np.arange(BY)) @ inverse, planes)
+
+
+def null_planes(planes, totals):
+    inverse = null_inverse()
+    v = [weigh(inverse[i], planes) - (totals[0] + (-1.0) ** i * totals[1]) / float(NY) for i in range(BY)]
+    return [weigh(-inverse[:, p] / float(NX * NZ), v) for p in range(16)]
+
+
+def tails(z):
+    return TAIL * RATIO / (1.0 - RATIO * z), TAIL * RATIO / (z - RATIO)
+
+
+def couple_blocks(place, m, cycle, out, hold):
+    ratio = [cycle[0, 0, 0, 8 * t:8 * t + 8, :] for t in range(3)]
+    close = [cycle[0, 0, 1, 8 * t:8 * t + 8, :] for t in range(3)]
+    upper = lax.broadcasted_iota(jnp.int32, (8, 128), 0) < 4
+
+    def advance(j, s):
+        new = []
+        for t in range(3):
+            rows = slice(8 * t, 8 * t + 8)
+            new.append(ratio[t] * s[t] + jnp.where(upper, m[j, rows, :], m[ROWS - 1 - j, rows, :]))
+        return tuple(new)
+
+    zero = jnp.zeros((8, 128), F32)
+    s = lax.fori_loop(0, ROWS, advance, (zero,) * 3, unroll=4)
+    s = tuple(s[t] * close[t] for t in range(3))
+
+    def store(j, s):
+        for t in range(3):
+            hold[j, 8 * t:8 * t + 8, :] = s[t]
+        return advance(j, s)
+
+    lax.fori_loop(0, ROWS, store, s, unroll=4)
+
+    def merge(j, carry):
+        for t in range(3):
+            rows = slice(8 * t, 8 * t + 8)
+            out[j, rows, :] = jnp.where(upper, hold[j, rows, :], hold[ROWS - 1 - j, rows, :])
+        return carry
+
+    lax.fori_loop(0, ROWS, merge, 0, unroll=4)
+
+
+def backward_z(s, keep, wh, wl, out, made):
+    def step(j, carry):
+        for t in range(3):
+            at = lambda p: keep[p, t, pl.ds(8 * j, 8), :]
+            state = lambda m: s[pl.ds(192 * j + 8 * t + m, 8, stride=24), :]
+            q = [at(p) for p in range(BY)]
+            plus, minus, last, first = [at(BY + p) for p in range(4)]
+            p = [0.0] * BY
+            g = [0.0] * 4
+            for k in range(4):
+                z, a = at(16 + k), at(20 + k)
+                near, far = tails(z)
+                from_left, from_right = state(k), state(4 + k)
+                right = from_left - z * (near * minus + EDGE * first)
+                left = from_right + z * (near * plus + EDGE * last)
+                for i in range(BY):
+                    right = (right if i == 0 else z * right) + q[i]
+                    p[i] = p[i] - a * right
+                    back = BY - 1 - i
+                    p[back] = p[back] - a * left
+                    left = z * (left + q[back])
+                right = z * right + (z * far * plus + EDGE * last)
+                left = left - (z * far * minus + EDGE * first)
+                inverse = 1.0 / z
+                g[0] = g[0] - a * (near * right + far * from_right)
+                g[1] = g[1] + a * (near * left + far * from_left)
+                g[2] = g[2] - a * EDGE * (right + inverse * from_right)
+                g[3] = g[3] + a * EDGE * (left + inverse * from_left)
+            for i, value in enumerate(p + g):
+                made[i, t, pl.ds(8 * j, 8), :] = value
+        return carry
+
+    lax.fori_loop(0, ROWS // 8, step, 0)
+    for t in range(2):
+        null = keep[20, t, 0:8, :] == 0.0
+        planes = [keep[p, t, 0:8, :] for p in range(16)]
+        own = null_sums(planes)
+        state = lambda m: s[pl.ds(8 * t + m, 8, stride=24), :]
+        totals = [(own[k] + state(k) + state(4 + k)) / 3.0 for k in range(2)]
+        for i, value in enumerate(null_planes(planes, totals)):
+            made[i, t, 0:8, :] = jnp.where(null, value, made[i, t, 0:8, :])
     total = None
     for y in range(8):
         planes = (y, 6 + y) if y < 6 else (6 + y, 8 + y)
-        t = [[x[pl.ds(16 * k + p, 64, stride=48), :] for k in range(3)] for p in planes]
+        t = [[made[p, k] for k in range(3)] for p in planes]
         low = jnp.concatenate([t[0][0], t[1][0], join(t[0][2], t[1][2])], 1)
         high = jnp.concatenate([t[0][1], t[1][1], join_high(t[0][2], t[1][2])], 1)
         z = two(jnp.concatenate([low, high], 0))
@@ -253,25 +421,17 @@
         out[c, 256:280, :] = total[c * 24:(c + 1) * 24]
 
 
-def solve_y(x, kappa2, wave2, ah, al, bh, bl, out):
-    tiles = [x[:, 16 * t:16 * (t + 1), :].reshape(ROWS * 16, 128) for t in range(3)]
-    s = dot3((ah[...], al[...]), two(jnp.concatenate(tiles, 1)))
-    den = wave2[...] + kappa2[...]
-    null = den == 0.0
-    s = jnp.where(null, 0.0, -s / (jnp.where(null, 1.0, den) * float(NX * NY * NZ)))
-    r = dot3((bh[...], bl[...]), two(s))
-    for t in range(3):
-        out[:, 16 * t:16 * (t + 1), :] = r[:, 128 * t:128 * (t + 1)].reshape(ROWS, 16, 128)
-
-
-def call(kernel, out_shape, args, scratch=(), scalars=0, flops=10**9):
+def call(kernel, out_shape, args, scratch=(), scalars=0, anywhere=()):
     spec_v = pl.BlockSpec(memory_space=pltpu.VMEM)
     spec_s = pl.BlockSpec(memory_space=pltpu.SMEM)
     many = isinstance(out_shape, (tuple, list))
     return pl.pallas_call(
         kernel,
         out_shape=out_shape,
-        in_specs=[spec_s] * scalars + [spec_v] * (len(args) - scalars),
+        in_specs=[
+            spec_s if i < scalars else pl.BlockSpec(memory_space=pl.ANY) if i in anywhere else spec_v
+            for i in range(len(args))
+        ],
         out_specs=[spec_v] * len(out_shape) if many else spec_v,
         scratch_shapes=list(scratch),
         compiler_params=pltpu.CompilerParams(vmem_limit_bytes=48 * 2**20),
@@ -293,23 +453,29 @@
         [pltpu.VMEM(flat, F32), pltpu.VMEM((560, NX), BF16), pltpu.VMEM((560, NX), BF16)], 3,
     )
     x = lax.all_to_all(x, "col", 0, 0, tiled=True)
-    x = call(forward_z, sds((ROWS * 48, 128), F32), [x, *k["wz"]])
-    x = lax.all_to_all(x.reshape(ROWS, 48, 128), "row", 0, 0, tiled=True)
-    wx2, wy2, wz2 = [jnp.asarray(a) for a in k["wave2"]]
-    x128 = lax.dynamic_slice_in_dim(wx2, 128 * col, 128)
-    x64 = lax.dynamic_slice_in_dim(wx2, 512 + 64 * col, 64)
-    z0 = lax.dynamic_slice_in_dim(wz2, row, 1)
-    z1 = lax.dynamic_slice_in_dim(wz2, 64 + row, 1)
-    kappa2 = jnp.concatenate([x128 + z0, x128 + z1, x64 + z0, x64 + z1]).reshape(1, 384)
-    x = call(solve_y, sds((ROWS, 48, 128), F32), [x, kappa2, wy2.reshape(NY, 1), *k["wy"], *k["wy_t"]])
-    x = lax.all_to_all(x, "row", 0, 0, tiled=True).reshape(ROWS * 48, 128)
-    x = call(backward_z, sds(mov, F32), [x, *k["wz_t"]])
+    m, keep = call(
+        forward_z, (sds((ROWS * 24, 128), F32), sds((24, 3, ROWS, 128), F32)),
+        [place, x, *k["wz"], k["local"]], [pltpu.SemaphoreType.DMA], 1, anywhere=(4,),
+    )
+    m = lax.all_to_all(m.reshape(ROWS, 24, 128), "row", 0, 0, tiled=True)
+    m = pl.pallas_call(
+        couple_blocks, out_shape=sds((ROWS, 24, 128), F32),
+        grid_spec=pltpu.PrefetchScalarGridSpec(
+            num_scalar_prefetch=1, grid=(1,),
+            in_specs=[pl.BlockSpec((ROWS, 24, 128), lambda i, p: (0, 0, 0)),
+                      pl.BlockSpec((1, 1, 2, 24, 128), lambda i, p: (p[1], p[0], 0, 0, 0))],
+            out_specs=pl.BlockSpec((ROWS, 24, 128), lambda i, p: (0, 0, 0)),
+            scratch_shapes=[pltpu.VMEM((ROWS, 24, 128), F32)],
+        ),
+        name="couple_blocks",
+    )(place, m, k["cycle"])
+    m = lax.all_to_all(m, "row", 0, 0, tiled=True).reshape(ROWS * 24, 128)
+    x = call(backward_z, sds(mov, F32), [m, keep, *k["wz_t"]], [pltpu.VMEM((16, 3, ROWS, 128), F32)])
     x = lax.all_to_all(x, "col", 0, 0, tiled=True)
     outs = call(
         backward_x, [sds(flat, F32)] * 3,
         [place, inflow_cells, inflow_speed, *fields, x, *k["left_t"], *k["hx"], *k["bwd_dx"]],
-        [pltpu.VMEM(flat, F32), pltpu.VMEM((560, NX), BF16), pltpu.VMEM((560, NX), BF16),
-         pltpu.VMEM((8, 128), F32), pltpu.VMEM((8, 128), F32)], 3,
+        [pltpu.VMEM(flat, F32), pltpu.VMEM((560, NX), BF16), pltpu.VMEM((560, NX), BF16)], 3,
     )
     return tuple(o.reshape(BY, BZ, NX) for o in outs)
 

time: 201 us -> 165 us (0.82)
  waiting for transfers between devices: 33.8 us -> 0 us
  blocking collectives: 103 us -> 121 us
  starting transfers between devices: 12.7 us -> 0 us
  other arithmetic: 4.26 us -> 0.08 us
  Pallas kernels: 37.3 us -> 34.8 us
    all_to_all x1 -> x0, waiting for transfers between devices: 33.8 us -> none  [body(): x = lax.all_to_all(x.reshape(ROWS, 48, 128), 'row', 0, 0, tiled=True)]
    all_to_all x1 -> x2, blocking collectives: 45.6 us -> 63.5 us  [the longest x1 34.9 us: body(): m = lax.all_to_all(m.reshape(ROWS, 24, 128), 'row', 0, 0, tiled=True)]
    all_to_all x1 -> x0, starting transfers between devices: 12.7 us -> none  [body(): x = lax.all_to_all(x.reshape(ROWS, 48, 128), 'row', 0, 0, tiled=True)]
    add x2 -> x0, other arithmetic: 4.11 us -> none  [the longest x1 2.05 us: body(): x128 + z0]
    pallas_call x5, Pallas kernels: 37.3 us -> 34.8 us  [the longest x4 31.7 us: call(): pl.pallas_call(kernel, out_shape=out_shape, in_specs=[spec_s if i < scala...]
    unnamed x42 -> x40, local copies, waits for them, and re-layouts: 7.63 us -> 7.63 us
  transfers between devices with their start and end apart: 1 -> 0, of which waited for: 1 -> 0; matrix products, arithmetic and copies ran while one was open for 2% -> 0% of each run, Pallas kernels for 0% -> 0%
where the time goes in v2:
time: 165 us
  blocking collectives  121 us (73%)
  Pallas kernels  34.8 us (21%)
  local copies, waits for them, and re-layouts  7.63 us (5%)
    all_to_all x2, blocking collectives, body(): x = lax.all_to_all(x, 'col', 0, 0, tiled=True)  57.8 us
    all_to_all x1, blocking collectives, body(): m = lax.all_to_all(m.reshape(ROWS, 24, 128), 'row', 0, 0, tiled=True)  34.9 us
    pallas_call x4, Pallas kernels, call(): pl.pallas_call(kernel, out_shape=out_shape, in_specs=[spec_s if i < scala...  31.7 us
    all_to_all x1, blocking collectives, body(): m = lax.all_to_all(m, 'row', 0, 0, tiled=True).reshape(ROWS * 24, 128)  28.6 us
    unnamed x40, local copies, waits for them, and re-layouts  7.63 us

profile of v2, /device:TPU:1, one launch (start us, length us, event | category | flops | bytes accessed | tf_op | source)
XLA Modules:
  0.0 164.5 jit_solution(6471696620234433684)
XLA Ops:
  0.6 0.1 pad_add_fusion.place
  0.7 1.3 copy-done
  2.0 1.3 copy-done.2
  3.3 1.3 copy-done.4
  4.5 1.2 copy-done.8
  5.7 1.2 copy-done.9
  6.8 0.7 copy-done.14
  7.6 0.7 copy-done.16
  8.3 12.8 %forward_x.1 = f32[4,280,384]{2,1,0:T(8,128)} custom-call(s32[2]{0:T(128)S(1)} %pad_add_fusion.place, s32[4096]{0:T(1024)S(1)} %copy-done.14, f32[4096]{0:T(1024)S(1)} %copy-done.16, f32[384,768]{1,0:T(8,128)S(1)} %bitcast.11, f32[384,768]{1,0:T(8,128)S(1)} %bitcast.13, f32[384,768]{1,0:T(8,128)S(1)} %bitcast.15, s32[384,768]{1,0:T(8,128)} %bitcast.19, ...), custom_call_target="tpu_custom_call" | custom-call | tf_op jit(solution)/shard_map/forward_x/pallas_call | solution.py:428
  21.1 28.1 %all_to_all.20.x = f32[4,280,384]{2,1,0:T(8,128)S(1)} all-to-all(f32[4,280,384]{2,1,0:T(8,128)} %forward_x.1), channel_id=1, replica_groups=mesh['row'=64,'col'=4] {'col'}, dimensions={0} | all-to-all | bytes 3440640 | tf_op jit(solution)/shard_map/all_to_all | solution.py:455
  49.2 0.0 copy-done.18
  49.2 2.7 %forward_z.1 = (f32[1536,128]{1,0:T(8,128)S(1)}, f32[24,3,64,128]{3,2,1,0:T(8,128)S(1)}) custom-call(s32[2]{0:T(128)S(1)} %pad_add_fusion.place, f32[4,280,384]{2,1,0:T(8,128)S(1)} %all_to_all.20.x, bf16[6,128,224]{2,1,0:T(8,128)(2,1)S(1)} %copy-done.11, bf16[6,128,224]{2,1,0:T(8,128)(2,1)S(1)} %copy-done.10, f32[4,8,3,64,128]{4,3,2,1,0:T(8,128)} %constant.49.clone.table), custom_call_target="tpu_custom_call" | custom-call | tf_op jit(solution)/shard_map/forward_z/pallas_call | solution.py:428
  52.0 34.9 %all_to_all.21.m = f32[64,24,128]{2,1,0:T(8,128)} all-to-all(f32[64,24,128]{2,1,0:T(8,128)S(1)} %bitcast.18), channel_id=1, replica_groups=mesh['row'=64,'col'=4] {'row'}, dimensions={0} | all-to-all | bytes 1572864 | tf_op jit(solution)/shard_map/all_to_all | solution.py:460
  86.8 3.2 %couple_blocks.1 = f32[64,24,128]{2,1,0:T(8,128)} custom-call(s32[2]{0:T(128)} %copy-done.18, f32[64,24,128]{2,1,0:T(8,128)} %all_to_all.21.m, f32[4,64,2,24,128]{4,3,2,1,0:T(8,128)} %constant.50.clone.cycle), custom_call_target="tpu_custom_call" | custom-call | tf_op jit(solution)/shard_map/couple_blocks/pallas_call | solution.py:461
  90.0 28.6 %all_to_all.22 = f32[64,24,128]{2,1,0:T(8,128)S(1)} all-to-all(f32[64,24,128]{2,1,0:T(8,128)} %couple_blocks.1), channel_id=1, replica_groups=mesh['row'=64,'col'=4] {'row'}, dimensions={0} | all-to-all | bytes 1572864 | tf_op jit(solution)/shard_map/all_to_all | solution.py:472
  118.6 3.2 %backward_z.1 = f32[4,280,384]{2,1,0:T(8,128)S(1)} custom-call(f32[1536,128]{1,0:T(8,128)S(1)} %bitcast.17, f32[24,3,64,128]{3,2,1,0:T(8,128)S(1)} %get-tuple-element.9.keep, bf16[6,224,128]{2,1,0:T(8,128)(2,1)S(1)} %copy-done.13, bf16[6,224,128]{2,1,0:T(8,128)(2,1)S(1)} %copy-done.12), custom_call_target="tpu_custom_call" | custom-call | tf_op jit(solution)/shard_map/backward_z/pallas_call | solution.py:428
  121.9 0.0 copy-start.1
  121.9 0.0 copy-start.3
  121.9 0.0 copy-start.6
  121.9 0.0 copy-start.15
  121.9 0.0 copy-start.17
  121.9 0.0 copy-start.19
  121.9 29.7 %all_to_all.23.x = f32[4,280,384]{2,1,0:T(8,128)} all-to-all(f32[4,280,384]{2,1,0:T(8,128)S(1)} %backward_z.1), channel_id=1, replica_groups=mesh['row'=64,'col'=4] {'col'}, dimensions={0} | all-to-all | bytes 3440640 | tf_op jit(solution)/shard_map/all_to_all | solution.py:474
  151.7 12.9 %backward_x.1 = (f32[384,768]{1,0:T(8,128)}, f32[384,768]{1,0:T(8,128)}, f32[384,768]{1,0:T(8,128)}) custom-call(s32[2]{0:T(128)S(1)} %copy-done.19, s32[4096]{0:T(1024)S(1)} %copy-done.15, f32[4096]{0:T(1024)S(1)} %copy-done.17, f32[384,768]{1,0:T(8,128)S(1)} %bitcast.12, f32[384,768]{1,0:T(8,128)S(1)} %bitcast.14, f32[384,768]{1,0:T(8,128)S(1)} %bitcast.16, ...), custom_call_target="tpu_custom_call" | custom-call | tf_op jit(solution)/shard_map/backward_x/pallas_call | solution.py:428
  (26 shorter events, 0.0 us)
Async XLA Ops:
  0.7 48.5 %copy-start.18 = (s32[2]{0:T(128)}, s32[2]{0:T(128)S(1)}, u32[]{:S(2)}) copy-start(s32[2]{0:T(128)S(1)} %pad_add_fusion.place) | copy-start | bytes 28
  0.7 1.3 copy-start
  2.0 1.3 copy-start.2
  3.3 1.3 copy-start.4
  4.5 1.2 copy-start.8
  5.7 1.2 copy-start.9
  6.8 0.7 copy-start.14
  7.6 0.7 copy-start.16
  21.1 28.1 %copy-start.10 = (bf16[6,128,224]{2,1,0:T(8,128)(2,1)S(1)}, bf16[6,128,224]{2,1,0:T(8,128)(2,1)}, u32[]{:S(2)}) copy-start(bf16[6,128,224]{2,1,0:T(8,128)(2,1)} %constant.48.clone.wl) | copy-start | bytes 1032196
  21.1 28.1 %copy-start.11 = (bf16[6,128,224]{2,1,0:T(8,128)(2,1)S(1)}, bf16[6,128,224]{2,1,0:T(8,128)(2,1)}, u32[]{:S(2)}) copy-start(bf16[6,128,224]{2,1,0:T(8,128)(2,1)} %constant.47.clone.wh) | copy-start | bytes 1032196
  90.0 28.6 %copy-start.12 = (bf16[6,224,128]{2,1,0:T(8,128)(2,1)S(1)}, bf16[6,224,128]{2,1,0:T(8,128)(2,1)}, u32[]{:S(2)}) copy-start(bf16[6,224,128]{2,1,0:T(8,128)(2,1)} %constant.52.clone.wl) | copy-start | bytes 1032196
  90.0 28.6 %copy-start.13 = (bf16[6,224,128]{2,1,0:T(8,128)(2,1)S(1)}, bf16[6,224,128]{2,1,0:T(8,128)(2,1)}, u32[]{:S(2)}) copy-start(bf16[6,224,128]{2,1,0:T(8,128)(2,1)} %constant.51.clone.wh) | copy-start | bytes 1032196
  118.6 33.0 %copy-start.5 = (f32[12,32,768]{2,1,0:T(8,128)S(1)}, f32[12,32,768]{2,1,0:T(8,128)}, u32[]{:S(2)}) copy-start(f32[12,32,768]{2,1,0:T(8,128)} %param.24) | copy-start | bytes 3538948
  118.6 33.0 %copy-start.7 = (bf16[768,560]{1,0:T(8,128)(2,1)S(1)}, bf16[768,560]{1,0:T(8,128)(2,1)}, u32[]{:S(2)}) copy-start(bf16[768,560]{1,0:T(8,128)(2,1)} %constant.53.clone.lh) | copy-start | bytes 2580484
  121.9 29.8 %copy-start.1 = (f32[12,32,768]{2,1,0:T(8,128)S(1)}, f32[12,32,768]{2,1,0:T(8,128)}, u32[]{:S(2)}) copy-start(f32[12,32,768]{2,1,0:T(8,128)} %param.22) | copy-start | bytes 3538948
  121.9 29.8 %copy-start.3 = (f32[12,32,768]{2,1,0:T(8,128)S(1)}, f32[12,32,768]{2,1,0:T(8,128)}, u32[]{:S(2)}) copy-start(f32[12,32,768]{2,1,0:T(8,128)} %param.23) | copy-start | bytes 3538948
  121.9 29.7 %copy-start.6 = (bf16[768,560]{1,0:T(8,128)(2,1)S(1)}, bf16[768,560]{1,0:T(8,128)(2,1)}, u32[]{:S(2)}) copy-start(bf16[768,560]{1,0:T(8,128)(2,1)} %constant.54.clone.ll) | copy-start | bytes 2580484
  121.9 29.7 %copy-start.15 = (s32[4096]{0:T(1024)S(1)}, s32[4096]{0:T(1024)}, u32[]{:S(2)}) copy-start(s32[4096]{0:T(1024)} %cells.3) | copy-start | bytes 49156
  121.9 29.7 %copy-start.17 = (f32[4096]{0:T(1024)S(1)}, f32[4096]{0:T(1024)}, u32[]{:S(2)}) copy-start(f32[4096]{0:T(1024)} %speed.3) | copy-start | bytes 49156
  121.9 29.7 %copy-start.19 = (s32[2]{0:T(128)S(1)}, s32[2]{0:T(128)}, u32[]{:S(2)}) copy-start(s32[2]{0:T(128)} %copy-done.18) | copy-start | bytes 28

commit v3 on v2

--- a/solution.py
+++ b/solution.py
@@ -63,6 +63,24 @@
     return dense, local, moments, far
 
 
+THIRD = NX // 3
+ROOT = np.sqrt(3.0)
+
+
+def thirds_forward(m):
+    rows = [m[:THIRD, 0::3]]
+    for r in (1, 2):
+        top = m[:THIRD, r::3]
+        rows += [top, (2.0 * m[THIRD:2 * THIRD, r::3] + top) / ROOT]
+    return np.concatenate(rows, 0)
+
+
+def thirds_backward(m):
+    top = np.concatenate([m[1::3, :THIRD], m[2::3, :THIRD]], 0)
+    next_third = np.concatenate([m[1::3, THIRD:2 * THIRD], m[2::3, THIRD:2 * THIRD]], 0)
+    return np.concatenate([m[0::3, :THIRD], top, (2.0 * next_third + top) / ROOT], 0)
+
+
 def halves(a):
     a = np.asarray(a, np.float32)
     hi = a.astype(jnp.bfloat16)
@@ -75,7 +93,7 @@
 
 
 def mode_tables():
-    wx, wz = wave(NX), wave(NZ)
+    wx, wz = wave(NX)[np.arange(NX).reshape(256, 3).T.reshape(-1)], wave(NZ)
     kappa = np.sqrt(wz[:, None] ** 2 + wx[None, :] ** 2).reshape(-1)
     null = kappa == 0.0
     kap = np.where(null, 1.0, kappa)
@@ -129,14 +147,8 @@
     eye_y, eye_z = np.eye(BY), np.eye(BZ)
     lv_q, lv_m = np.kron(loc_y, eye_z), np.kron(mom_y, eye_z)
     lw_q, lw_m = np.kron(eye_y, loc_z), np.kron(eye_y, mom_z)
-    parts = []
-    for h in range(2):
-        parts.append(np.concatenate([lv_q[h * 192:(h + 1) * 192], lw_q[h * 192:(h + 1) * 192]], 1))
-        vm = lv_m[h * 64:(h + 1) * 64]
-        parts.append(np.concatenate([vm, np.zeros_like(vm)], 1))
-        wm = lw_m[h * 24:(h + 1) * 24]
-        parts.append(np.concatenate([np.zeros_like(wm), wm], 1))
-    left = np.concatenate(parts, 0)
+    left_v = np.concatenate([lv_m, lv_q, np.zeros_like(lw_m)], 0)
+    left_w = np.concatenate([np.zeros_like(lv_m), lw_q, lw_m], 0)
     far_hz = np.einsum("kz,zcm->kcm", hz, far_z)
     wz = np.zeros((6, NZ, 224))
     for y in range(6):
@@ -146,11 +158,13 @@
         wz[y, :, NZ:] = wide.reshape(NZ, 96)
     out = {}
     for name, value in (
-        ("hx", hx),
-        ("fwd_dx", dense_x.T @ hx),
-        ("bwd_dx", hx @ dense_x.T),
-        ("left", left),
-        ("left_t", left.T),
+        ("hx", thirds_forward(hx)),
+        ("fwd_dx", thirds_forward(dense_x.T @ hx)),
+        ("hx_back", thirds_backward(hx)),
+        ("bwd_dx", thirds_backward(hx @ dense_x.T)),
+        ("left", np.concatenate([left_v, left_w], 1)),
+        ("left_tv", left_v[:512].T),
+        ("left_tw", left_w[128:].T),
         ("wz", wz),
         ("wz_t", np.swapaxes(wz, 1, 2)),
     ):
@@ -202,28 +216,52 @@
     lax.fori_loop(0, 2 * BY, step, 0)
 
 
-def forward_x(place, cells, speed, u, v, w, solid, lh, ll, hh, hl, dh, dl, out, upward, sh, sl):
+def fold(parts):
+    a, b, c = parts
+    return a + (b + c), a - 0.5 * (b + c), (0.5 * ROOT).item() * (b - c)
+
+
+def unfold(a, b, q):
+    low, high = a - 0.5 * b, (0.5 * ROOT).item() * q
+    return a + b, low + high, low - high
+
+
+def forward_x(place, cells, speed, u_in, v_in, w_in, solid_in, lh_in, ll_in, hh_in, hl_in, dh_in, dl_in,
+              out, u, v, w, solid, lh, ll, hh, hl, dh, dl, sems):
+    pairs = [(solid_in, solid), (w_in, w), (lh_in, lh), (ll_in, ll), (v_in, v),
+             (hh_in, hh), (hl_in, hl), (u_in, u), (dh_in, dh), (dl_in, dl)]
+    copies = [pltpu.make_async_copy(a, b, sems.at[i]) for i, (a, b) in enumerate(pairs)]
+    for copy in copies:
+        copy.start()
+    for copy in copies[:2]:
+        copy.wait()
     fluid = (1 - solid[...]).astype(F32)
-    upward[...] = w[...] * fluid
-    set_inflow(place, cells, speed, upward)
-    u2 = two(u[...] * fluid)
+    w[...] = w[...] * fluid
+    set_inflow(place, cells, speed, w)
+    for copy in copies[2:5]:
+        copy.wait()
     left = (lh[...], ll[...])
+    thirds = []
     for n in range(3):
         at = slice(n * 256, (n + 1) * 256)
-        both = jnp.concatenate([v[:, at] * fluid[:, at], upward[:, at]], 0)
-        s = dot3(left, two(both))
-        hi, lo = two(s)
-        sh[:, at] = hi
-        sl[:, at] = lo
-    s2 = (sh[...], sl[...])
+        both = jnp.concatenate([v[:, at] * fluid[:, at], w[:, at]], 0)
+        thirds.append(dot3(left, two(both)))
+    c0, c, d = fold(thirds)
+    all_0, all_1 = two(c0), two(jnp.concatenate([c, d], 1))
+    for copy in copies[5:8]:
+        copy.wait()
+    c0, c, d = fold([u[:, n * 256:(n + 1) * 256] * fluid[:, n * 256:(n + 1) * 256] for n in range(3)])
+    east_0, east_1 = two(c0), two(jnp.concatenate([c, d], 1))
+    for copy in copies[8:]:
+        copy.wait()
     for n in range(3):
-        at = slice(n * 256, (n + 1) * 256)
-        r = dot3(s2, (hh[:, at], hl[:, at]))
-        d = dot3(u2, (dh[:, at], dl[:, at]))
-        top = jnp.concatenate([r[:192] + d[:192], r[192:280]], 0)
-        bottom = jnp.concatenate([r[280:472] + d[192:], r[472:]], 0)
+        at = slice(0, 256) if n == 0 else slice(512 * n - 256, 512 * n + 256)
+        r = dot3(all_1 if n else all_0, (hh[at, :], hl[at, :]))
+        d = dot3(east_1 if n else east_0, (dh[at, :], dl[at, :]))
         for t in range(2):
-            a, b = top[:, t * 128:(t + 1) * 128], bottom[:, t * 128:(t + 1) * 128]
+            own = slice(t * 128, (t + 1) * 128)
+            a = jnp.concatenate([r[128:320, own] + d[:192, own], r[0:64, own], r[512:536, own]], 0)
+            b = jnp.concatenate([r[320:512, own] + d[192:, own], r[64:128, own], r[536:560, own]], 0)
             c = 2 * n + t
             if c < 4:
                 out[c, :, 0:128] = a
@@ -234,7 +272,8 @@
                 out[c + 1, :, 256:384] = join_high(a, b)
 
 
-def backward_x(place, cells, speed, u, v, w, solid, x, lh, ll, hh, hl, dh, dl, uo, vo, wo, upward, th, tl):
+def backward_x(place, cells, speed, u, v, w, solid, x, vh, vl, wh, wl, hh, hl, dh, dl,
+               uo, vo, wo, upward, th, tl, us, vs, ws, sems):
     fluid = (1 - solid[...]).astype(F32)
     upward[...] = w[...] * fluid
     set_inflow(place, cells, speed, upward)
@@ -245,20 +284,40 @@
             c = 2 * (t - 4)
             e, o = x[c, :, 256:384], x[c + 1, :, 256:384]
             a, b = join(e, o), join_high(e, o)
-        hi, lo = two(jnp.concatenate([a, b], 0))
+        rows = [a[192:256], b[192:256], a[0:192], b[0:192], a[256:280], b[256:280]]
+        hi, lo = two(jnp.concatenate(rows, 0))
         th[:, t * 128:(t + 1) * 128] = hi
         tl[:, t * 128:(t + 1) * 128] = lo
-    t2 = (th[...], tl[...])
-    left = (lh[...], ll[...])
+
+    def back(rows, mh, ml):
+        first, rest = (th[rows, 0:256], tl[rows, 0:256]), (th[rows, 256:768], tl[rows, 256:768])
+        return unfold(*[
+            dot3(left, (mh[at, :], ml[at, :]))
+            for left, at in ((first, slice(0, 256)), (rest, slice(256, 768)), (rest, slice(768, 1280)))
+        ])
+
+    p = back(slice(0, 560), hh, hl)
+    d = back(slice(128, 512), dh, dl)
+    copies = []
+
+    def send(i, n, stage, target):
+        at = pl.ds(n * 256, 256)
+        copies.append(pltpu.make_async_copy(stage.at[:, at], target.at[:, at], sems.at[3 * i + n]))
+        copies[-1].start()
+
     for n in range(3):
         at = slice(n * 256, (n + 1) * 256)
-        p = dot3(t2, (hh[:, at], hl[:, at]))
-        d = dot3(t2, (dh[:, at], dl[:, at]))
-        uo[0:192, at] = u[0:192, at] * fluid[0:192, at] - d[0:192]
-        uo[192:384, at] = u[192:384, at] * fluid[192:384, at] - d[280:472]
-        g = dot3(left, two(p))
-        vo[:, at] = v[:, at] * fluid[:, at] + g[0:384]
-        wo[:, at] = upward[:, at] + g[384:768]
+        us[:, at] = u[:, at] * fluid[:, at] - d[n]
+        send(0, n, us, uo)
+    for n in range(3):
+        at = slice(n * 256, (n + 1) * 256)
+        hi, lo = two(p[n])
+        vs[:, at] = v[:, at] * fluid[:, at] + dot3((vh[...], vl[...]), (hi[0:512], lo[0:512]))
+        send(1, n, vs, vo)
+        ws[:, at] = upward[:, at] + dot3((wh[...], wl[...]), (hi[128:560], lo[128:560]))
+        send(2, n, ws, wo)
+    for copy in copies:
+        copy.wait()
 
 
 def forward_z(place, x, wh, wl, table, out, keep, sem):
@@ -421,7 +480,7 @@
         out[c, 256:280, :] = total[c * 24:(c + 1) * 24]
 
 
-def call(kernel, out_shape, args, scratch=(), scalars=0, anywhere=()):
+def call(kernel, out_shape, args, scratch=(), scalars=0, anywhere=(), out_space=pltpu.VMEM, vmem=48):
     spec_v = pl.BlockSpec(memory_space=pltpu.VMEM)
     spec_s = pl.BlockSpec(memory_space=pltpu.SMEM)
     many = isinstance(out_shape, (tuple, list))
@@ -429,12 +488,12 @@
         kernel,
         out_shape=out_shape,
         in_specs=[
-            spec_s if i < scalars else pl.BlockSpec(memory_space=pl.ANY) if i in anywhere else spec_v
+            spec_s if i < scalars else pl.BlockSpec(memory_space=pltpu.HBM) if i in anywhere else spec_v
             for i in range(len(args))
         ],
-        out_specs=[spec_v] * len(out_shape) if many else spec_v,
+        out_specs=[pl.BlockSpec(memory_space=out_space)] * len(out_shape) if many else spec_v,
         scratch_shapes=list(scratch),
-        compiler_params=pltpu.CompilerParams(vmem_limit_bytes=48 * 2**20),
+        compiler_params=pltpu.CompilerParams(vmem_limit_bytes=vmem * 2**20),
         name=kernel.__name__,
     )(*args)
 
@@ -450,7 +509,8 @@
     x = call(
         forward_x, sds(mov, F32),
         [place, inflow_cells, inflow_speed, *fields, *k["left"], *k["hx"], *k["fwd_dx"]],
-        [pltpu.VMEM(flat, F32), pltpu.VMEM((560, NX), BF16), pltpu.VMEM((560, NX), BF16)], 3,
+        [pltpu.VMEM(flat, F32)] * 3 + [pltpu.VMEM(flat, jnp.int32)] + [pltpu.VMEM((560, NX), BF16)] * 2
+        + [pltpu.VMEM((1280, 256), BF16)] * 4 + [pltpu.SemaphoreType.DMA((10,))], 3, range(3, 13), vmem=60,
     )
     x = lax.all_to_all(x, "col", 0, 0, tiled=True)
     m, keep = call(
@@ -474,8 +534,9 @@
     x = lax.all_to_all(x, "col", 0, 0, tiled=True)
     outs = call(
         backward_x, [sds(flat, F32)] * 3,
-        [place, inflow_cells, inflow_speed, *fields, x, *k["left_t"], *k["hx"], *k["bwd_dx"]],
-        [pltpu.VMEM(flat, F32), pltpu.VMEM((560, NX), BF16), pltpu.VMEM((560, NX), BF16)], 3,
+        [place, inflow_cells, inflow_speed, *fields, x, *k["left_tv"], *k["left_tw"], *k["hx_back"], *k["bwd_dx"]],
+        [pltpu.VMEM(flat, F32), pltpu.VMEM((560, NX), BF16), pltpu.VMEM((560, NX), BF16)]
+        + [pltpu.VMEM(flat, F32)] * 3 + [pltpu.SemaphoreType.DMA((9,))], 3, out_space=pltpu.HBM,
     )
     return tuple(o.reshape(BY, BZ, NX) for o in outs)
 

time: 165 us -> 152 us (0.921)
  local copies, waits for them, and re-layouts: 7.63 us -> 0.1 us
  Pallas kernels: 34.8 us -> 28.9 us
    unnamed x40 -> x34, local copies, waits for them, and re-layouts: 7.63 us -> 0.1 us
    pallas_call x4, Pallas kernels: 31.7 us -> 25.7 us  [call(): pl.pallas_call(kernel, out_shape=out_shape, in_specs=[spec_s if i < scala...]
where the time goes in v3:
time: 152 us
  blocking collectives  121 us (80%)
  Pallas kernels  28.9 us (19%)
    all_to_all x2, blocking collectives, body(): x = lax.all_to_all(x, 'col', 0, 0, tiled=True)  57.8 us
    all_to_all x1, blocking collectives, body(): m = lax.all_to_all(m.reshape(ROWS, 24, 128), 'row', 0, 0, tiled=True)  34.9 us
    all_to_all x1, blocking collectives, body(): m = lax.all_to_all(m, 'row', 0, 0, tiled=True).reshape(ROWS * 24, 128)  28.6 us
    pallas_call x4, Pallas kernels, call(): pl.pallas_call(kernel, out_shape=out_shape, in_specs=[spec_s if i < scala...  25.7 us
    pallas_call x1, Pallas kernels, body(): pl.pallas_call(couple_blocks, out_shape=sds((ROWS, 24, 128), F32), grid_s...  3.19 us

profile of v3, /device:TPU:1, one launch (start us, length us, event | category | flops | bytes accessed | tf_op | source)
XLA Modules:
  0.0 151.8 jit_solution(11054358830971482801)
XLA Ops:
  0.6 0.6 pad_add_fusion.place
  1.2 10.9 %forward_x.1 = f32[4,280,384]{2,1,0:T(8,128)} custom-call(s32[2]{0:T(128)} %pad_add_fusion.place, s32[4096]{0:T(1024)} %cells.3, f32[4096]{0:T(1024)} %speed.3, f32[384,768]{1,0:T(8,128)} %bitcast.11, f32[384,768]{1,0:T(8,128)} %bitcast.15, f32[384,768]{1,0:T(8,128)} %bitcast.17, s32[384,768]{1,0:T(8,128)} %bitcast.19, ...), custom_call_target="tpu_custom_call" | custom-call | tf_op jit(solution)/shard_map/forward_x/pallas_call | solution.py:487
  12.2 0.0 copy-start.5
  12.2 0.0 copy-start.6
  12.2 0.0 copy-start.15
  12.2 28.1 %all_to_all.20.x = f32[4,280,384]{2,1,0:T(8,128)S(1)} all-to-all(f32[4,280,384]{2,1,0:T(8,128)} %forward_x.1), channel_id=1, replica_groups=mesh['row'=64,'col'=4] {'col'}, dimensions={0} | all-to-all | bytes 3440640 | tf_op jit(solution)/shard_map/all_to_all | solution.py:515
  40.3 2.7 %forward_z.1 = (f32[1536,128]{1,0:T(8,128)S(1)}, f32[24,3,64,128]{3,2,1,0:T(8,128)S(1)}) custom-call(s32[2]{0:T(128)S(1)} %copy-done.15, f32[4,280,384]{2,1,0:T(8,128)S(1)} %all_to_all.20.x, bf16[6,128,224]{2,1,0:T(8,128)(2,1)S(1)} %copy-done.6, bf16[6,128,224]{2,1,0:T(8,128)(2,1)S(1)} %copy-done.5, f32[4,8,3,64,128]{4,3,2,1,0:T(8,128)} %constant.57.clone.table), custom_call_target="tpu_custom_call" | custom-call | tf_op jit(solution)/shard_map/forward_z/pallas_call | solution.py:487
  43.0 34.9 %all_to_all.21.m = f32[64,24,128]{2,1,0:T(8,128)} all-to-all(f32[64,24,128]{2,1,0:T(8,128)S(1)} %bitcast.14), channel_id=1, replica_groups=mesh['row'=64,'col'=4] {'row'}, dimensions={0} | all-to-all | bytes 1572864 | tf_op jit(solution)/shard_map/all_to_all | solution.py:520
  77.9 3.2 %couple_blocks.1 = f32[64,24,128]{2,1,0:T(8,128)} custom-call(s32[2]{0:T(128)} %pad_add_fusion.place, f32[64,24,128]{2,1,0:T(8,128)} %all_to_all.21.m, f32[4,64,2,24,128]{4,3,2,1,0:T(8,128)} %constant.58.clone.cycle), custom_call_target="tpu_custom_call" | custom-call | tf_op jit(solution)/shard_map/couple_blocks/pallas_call | solution.py:521
  81.1 28.6 %all_to_all.22 = f32[64,24,128]{2,1,0:T(8,128)S(1)} all-to-all(f32[64,24,128]{2,1,0:T(8,128)} %couple_blocks.1), channel_id=1, replica_groups=mesh['row'=64,'col'=4] {'row'}, dimensions={0} | all-to-all | bytes 1572864 | tf_op jit(solution)/shard_map/all_to_all | solution.py:532
  109.7 0.0 copy-done.12
  109.7 0.0 copy-start.8
  109.7 0.0 copy-start.9
  109.7 0.0 copy-start.10
  109.7 3.2 %backward_z.1 = f32[4,280,384]{2,1,0:T(8,128)S(1)} custom-call(f32[1536,128]{1,0:T(8,128)S(1)} %bitcast.13, f32[24,3,64,128]{3,2,1,0:T(8,128)S(1)} %get-tuple-element.9.keep, bf16[6,224,128]{2,1,0:T(8,128)(2,1)S(1)} %copy-done.12, bf16[6,224,128]{2,1,0:T(8,128)(2,1)S(1)} %copy-done.11), custom_call_target="tpu_custom_call" | custom-call | tf_op jit(solution)/shard_map/backward_z/pallas_call | solution.py:487
  113.0 0.0 copy-start
  113.0 0.0 copy-start.1
  113.0 0.0 copy-start.2
  113.0 0.0 copy-start.3
  113.0 0.0 copy-start.13
  113.0 0.0 copy-start.14
  113.0 0.0 copy-start.16
  113.1 29.7 %all_to_all.23.x = f32[4,280,384]{2,1,0:T(8,128)} all-to-all(f32[4,280,384]{2,1,0:T(8,128)S(1)} %backward_z.1), channel_id=1, replica_groups=mesh['row'=64,'col'=4] {'col'}, dimensions={0} | all-to-all | bytes 3440640 | tf_op jit(solution)/shard_map/all_to_all | solution.py:534
  142.8 8.8 %backward_x.1 = (f32[384,768]{1,0:T(8,128)}, f32[384,768]{1,0:T(8,128)}, f32[384,768]{1,0:T(8,128)}) custom-call(s32[2]{0:T(128)S(1)} %copy-done.16, s32[4096]{0:T(1024)S(1)} %copy-done.13, f32[4096]{0:T(1024)S(1)} %copy-done.14, f32[384,768]{1,0:T(8,128)S(1)} %bitcast.12, f32[384,768]{1,0:T(8,128)} %bitcast.16, f32[384,768]{1,0:T(8,128)} %bitcast.18, ...), custom_call_target="tpu_custom_call" | custom-call | tf_op jit(solution)/shard_map/backward_x/pallas_call | solution.py:487
  (20 shorter events, 0.0 us)
Async XLA Ops:
  12.2 28.1 %copy-start.5 = (bf16[6,128,224]{2,1,0:T(8,128)(2,1)S(1)}, bf16[6,128,224]{2,1,0:T(8,128)(2,1)}, u32[]{:S(2)}) copy-start(bf16[6,128,224]{2,1,0:T(8,128)(2,1)} %constant.56.clone.wl) | copy-start | bytes 1032196
  12.2 28.1 %copy-start.6 = (bf16[6,128,224]{2,1,0:T(8,128)(2,1)S(1)}, bf16[6,128,224]{2,1,0:T(8,128)(2,1)}, u32[]{:S(2)}) copy-start(bf16[6,128,224]{2,1,0:T(8,128)(2,1)} %constant.55.clone.wh) | copy-start | bytes 1032196
  12.2 28.1 %copy-start.15 = (s32[2]{0:T(128)S(1)}, s32[2]{0:T(128)}, u32[]{:S(2)}) copy-start(s32[2]{0:T(128)} %pad_add_fusion.place) | copy-start | bytes 28
  81.1 28.6 %copy-start.11 = (bf16[6,224,128]{2,1,0:T(8,128)(2,1)S(1)}, bf16[6,224,128]{2,1,0:T(8,128)(2,1)}, u32[]{:S(2)}) copy-start(bf16[6,224,128]{2,1,0:T(8,128)(2,1)} %constant.60.clone.wl) | copy-start | bytes 1032196
  81.1 28.6 %copy-start.12 = (bf16[6,224,128]{2,1,0:T(8,128)(2,1)S(1)}, bf16[6,224,128]{2,1,0:T(8,128)(2,1)}, u32[]{:S(2)}) copy-start(bf16[6,224,128]{2,1,0:T(8,128)(2,1)} %constant.59.clone.wh) | copy-start | bytes 1032196
  109.7 33.1 %copy-start.4 = (bf16[1280,256]{1,0:T(8,128)(2,1)S(1)}, bf16[1280,256]{1,0:T(8,128)(2,1)}, u32[]{:S(2)}) copy-start(bf16[1280,256]{1,0:T(8,128)(2,1)} %constant.65.clone.hh) | copy-start | bytes 1966084
  109.7 33.1 %copy-start.7 = (bf16[384,432]{1,0:T(8,128)(2,1)S(1)}, bf16[384,432]{1,0:T(8,128)(2,1)}, u32[]{:S(2)}) copy-start(bf16[384,432]{1,0:T(8,128)(2,1)} %constant.64.clone.wl) | copy-start | bytes 995332
  109.7 33.1 %copy-start.8 = (bf16[384,432]{1,0:T(8,128)(2,1)S(1)}, bf16[384,432]{1,0:T(8,128)(2,1)}, u32[]{:S(2)}) copy-start(bf16[384,432]{1,0:T(8,128)(2,1)} %constant.63.clone.wh) | copy-start | bytes 995332
  109.7 33.0 %copy-start.9 = (bf16[384,512]{1,0:T(8,128)(2,1)S(1)}, bf16[384,512]{1,0:T(8,128)(2,1)}, u32[]{:S(2)}) copy-start(bf16[384,512]{1,0:T(8,128)(2,1)} %constant.62.clone.vl) | copy-start | bytes 1179652
  109.7 33.0 %copy-start.10 = (bf16[384,512]{1,0:T(8,128)(2,1)S(1)}, bf16[384,512]{1,0:T(8,128)(2,1)}, u32[]{:S(2)}) copy-start(bf16[384,512]{1,0:T(8,128)(2,1)} %constant.61.clone.vh) | copy-start | bytes 1179652
  113.0 29.8 %copy-start = (f32[12,32,768]{2,1,0:T(8,128)S(1)}, f32[12,32,768]{2,1,0:T(8,128)}, u32[]{:S(2)}) copy-start(f32[12,32,768]{2,1,0:T(8,128)} %param.26) | copy-start | bytes 3538948
  113.0 29.8 %copy-start.1 = (bf16[1280,256]{1,0:T(8,128)(2,1)S(1)}, bf16[1280,256]{1,0:T(8,128)(2,1)}, u32[]{:S(2)}) copy-start(bf16[1280,256]{1,0:T(8,128)(2,1)} %constant.68.clone.dl) | copy-start | bytes 1966084
  113.0 29.8 %copy-start.2 = (bf16[1280,256]{1,0:T(8,128)(2,1)S(1)}, bf16[1280,256]{1,0:T(8,128)(2,1)}, u32[]{:S(2)}) copy-start(bf16[1280,256]{1,0:T(8,128)(2,1)} %constant.67.clone.dh) | copy-start | bytes 1966084
  113.0 29.8 %copy-start.3 = (bf16[1280,256]{1,0:T(8,128)(2,1)S(1)}, bf16[1280,256]{1,0:T(8,128)(2,1)}, u32[]{:S(2)}) copy-start(bf16[1280,256]{1,0:T(8,128)(2,1)} %constant.66.clone.hl) | copy-start | bytes 1966084
  113.0 29.8 %copy-start.13 = (s32[4096]{0:T(1024)S(1)}, s32[4096]{0:T(1024)}, u32[]{:S(2)}) copy-start(s32[4096]{0:T(1024)} %cells.3) | copy-start | bytes 49156
  113.0 29.8 %copy-start.14 = (f32[4096]{0:T(1024)S(1)}, f32[4096]{0:T(1024)}, u32[]{:S(2)}) copy-start(f32[4096]{0:T(1024)} %speed.3) | copy-start | bytes 49156
  113.0 29.8 %copy-start.16 = (s32[2]{0:T(128)S(1)}, s32[2]{0:T(128)}, u32[]{:S(2)}) copy-start(s32[2]{0:T(128)} %pad_add_fusion.place) | copy-start | bytes 28

commit v4 on v3

--- a/solution.py
+++ b/solution.py
@@ -226,8 +226,23 @@
     return a + b, low + high, low - high
 
 
+def deal(place, blocks, outs):
+    for d, out in enumerate(outs):
+        out[...] = blocks[place[1] ^ d]
+
+
+def collect(place, ins, blocks):
+    for d, block in enumerate(ins):
+        blocks[place[1] ^ d] = block[...]
+
+
+def exchange(blocks):
+    moved = {d: lax.ppermute(blocks[d], "col", [(c, c ^ d) for c in range(COLS)]) for d in (2, 3, 1)}
+    return [blocks[0], moved[1], moved[2], moved[3]]
+
+
 def forward_x(place, cells, speed, u_in, v_in, w_in, solid_in, lh_in, ll_in, hh_in, hl_in, dh_in, dl_in,
-              out, u, v, w, solid, lh, ll, hh, hl, dh, dl, sems):
+              o0, o1, o2, o3, out, u, v, w, solid, lh, ll, hh, hl, dh, dl, sems):
     pairs = [(solid_in, solid), (w_in, w), (lh_in, lh), (ll_in, ll), (v_in, v),
              (hh_in, hh), (hl_in, hl), (u_in, u), (dh_in, dh), (dl_in, dl)]
     copies = [pltpu.make_async_copy(a, b, sems.at[i]) for i, (a, b) in enumerate(pairs)]
@@ -270,13 +285,15 @@
                 c = 2 * (c - 4)
                 out[c, :, 256:384] = join(a, b)
                 out[c + 1, :, 256:384] = join_high(a, b)
-
-
-def backward_x(place, cells, speed, u, v, w, solid, x, vh, vl, wh, wl, hh, hl, dh, dl,
-               uo, vo, wo, upward, th, tl, us, vs, ws, sems):
+    deal(place, out, (o0, o1, o2, o3))
+
+
+def backward_x(place, cells, speed, u, v, w, solid, x0, x1, x2, x3, vh, vl, wh, wl, hh, hl, dh, dl,
+               uo, vo, wo, x, upward, th, tl, us, vs, ws, sems):
     fluid = (1 - solid[...]).astype(F32)
     upward[...] = w[...] * fluid
     set_inflow(place, cells, speed, upward)
+    collect(place, (x0, x1, x2, x3), x)
     for t in range(6):
         if t < 4:
             a, b = x[t, :, 0:128], x[t, :, 128:256]
@@ -320,9 +337,10 @@
         copy.wait()
 
 
-def forward_z(place, x, wh, wl, table, out, keep, sem):
+def forward_z(place, x0, x1, x2, x3, wh, wl, table, out, keep, x, sem):
     copy = pltpu.make_async_copy(table.at[place[1]], keep.at[pl.ds(16, 8)], sem)
     copy.start()
+    collect(place, (x0, x1, x2, x3), x)
     marks = [x[c, 256:280, :] for c in range(COLS)]
     for y in range(8):
         own = [x[c, y * 32:(y + 1) * 32, :] for c in range(COLS)]
@@ -421,7 +439,7 @@
     lax.fori_loop(0, ROWS, merge, 0, unroll=4)
 
 
-def backward_z(s, keep, wh, wl, out, made):
+def backward_z(place, s, keep, wh, wl, o0, o1, o2, o3, out, made):
     def step(j, carry):
         for t in range(3):
             at = lambda p: keep[p, t, pl.ds(8 * j, 8), :]
@@ -478,6 +496,7 @@
             out[c, y * 32:(y + 1) * 32, :] = r[c * 32:(c + 1) * 32]
     for c in range(COLS):
         out[c, 256:280, :] = total[c * 24:(c + 1) * 24]
+    deal(place, out, (o0, o1, o2, o3))
 
 
 def call(kernel, out_shape, args, scratch=(), scalars=0, anywhere=(), out_space=pltpu.VMEM, vmem=48):
@@ -507,15 +526,15 @@
     sds = jax.ShapeDtypeStruct
     mov = (COLS, 280, 384)
     x = call(
-        forward_x, sds(mov, F32),
+        forward_x, [sds(mov[1:], F32)] * COLS,
         [place, inflow_cells, inflow_speed, *fields, *k["left"], *k["hx"], *k["fwd_dx"]],
-        [pltpu.VMEM(flat, F32)] * 3 + [pltpu.VMEM(flat, jnp.int32)] + [pltpu.VMEM((560, NX), BF16)] * 2
+        [pltpu.VMEM(mov, F32)] + [pltpu.VMEM(flat, F32)] * 3 + [pltpu.VMEM(flat, jnp.int32)] + [pltpu.VMEM((560, NX), BF16)] * 2
         + [pltpu.VMEM((1280, 256), BF16)] * 4 + [pltpu.SemaphoreType.DMA((10,))], 3, range(3, 13), vmem=60,
     )
-    x = lax.all_to_all(x, "col", 0, 0, tiled=True)
+    x = exchange(x)
     m, keep = call(
         forward_z, (sds((ROWS * 24, 128), F32), sds((24, 3, ROWS, 128), F32)),
-        [place, x, *k["wz"], k["local"]], [pltpu.SemaphoreType.DMA], 1, anywhere=(4,),
+        [place, *x, *k["wz"], k["local"]], [pltpu.VMEM(mov, F32), pltpu.SemaphoreType.DMA], 1, anywhere=(7,),
     )
     m = lax.all_to_all(m.reshape(ROWS, 24, 128), "row", 0, 0, tiled=True)
     m = pl.pallas_call(
@@ -530,12 +549,15 @@
         name="couple_blocks",
     )(place, m, k["cycle"])
     m = lax.all_to_all(m, "row", 0, 0, tiled=True).reshape(ROWS * 24, 128)
-    x = call(backward_z, sds(mov, F32), [m, keep, *k["wz_t"]], [pltpu.VMEM((16, 3, ROWS, 128), F32)])
-    x = lax.all_to_all(x, "col", 0, 0, tiled=True)
+    x = call(
+        backward_z, [sds(mov[1:], F32)] * COLS, [place, m, keep, *k["wz_t"]],
+        [pltpu.VMEM(mov, F32), pltpu.VMEM((16, 3, ROWS, 128), F32)], 1,
+    )
+    x = exchange(x)
     outs = call(
         backward_x, [sds(flat, F32)] * 3,
-        [place, inflow_cells, inflow_speed, *fields, x, *k["left_tv"], *k["left_tw"], *k["hx_back"], *k["bwd_dx"]],
-        [pltpu.VMEM(flat, F32), pltpu.VMEM((560, NX), BF16), pltpu.VMEM((560, NX), BF16)]
+        [place, inflow_cells, inflow_speed, *fields, *x, *k["left_tv"], *k["left_tw"], *k["hx_back"], *k["bwd_dx"]],
+        [pltpu.VMEM(mov, F32), pltpu.VMEM(flat, F32), pltpu.VMEM((560, NX), BF16), pltpu.VMEM((560, NX), BF16)]
         + [pltpu.VMEM(flat, F32)] * 3 + [pltpu.SemaphoreType.DMA((9,))], 3, out_space=pltpu.HBM,
     )
     return tuple(o.reshape(BY, BZ, NX) for o in outs)

time: 152 us -> 147 us (0.967)
  blocking collectives: 121 us -> 63.9 us
  waiting for transfers between devices: 0 us -> 38.5 us
  starting transfers between devices: 0 us -> 11.6 us
    all_to_all x2 -> x0, blocking collectives: 57.8 us -> none  [body(): x = lax.all_to_all(x, 'col', 0, 0, tiled=True)]
    ppermute x0 -> x6, waiting for transfers between devices: none -> 38.5 us  [exchange(): lax.ppermute(blocks[d], 'col', [(c, c ^ d) for c in range(COLS)])]
    ppermute x0 -> x6, starting transfers between devices: none -> 11.6 us  [exchange(): lax.ppermute(blocks[d], 'col', [(c, c ^ d) for c in range(COLS)])]
  transfers between devices with their start and end apart: 0 -> 6, of which waited for: 0 -> 4; matrix products, arithmetic and copies ran while one was open for 0% -> 0% of each run, Pallas kernels for 0% -> 0%
where the time goes in v4:
time: 147 us; the launch traced here: 146 us
  blocking collectives  63.9 us (43%)
  waiting for transfers between devices  38.5 us (26%)
  Pallas kernels  29.7 us (20%)
  starting transfers between devices  11.6 us (8%)
    ppermute x6, waiting for transfers between devices, exchange(): lax.ppermute(blocks[d], 'col', [(c, c ^ d) for c in range(COLS)])  38.5 us
    all_to_all x1, blocking collectives, body(): m = lax.all_to_all(m.reshape(ROWS, 24, 128), 'row', 0, 0, tiled=True)  35 us
    all_to_all x1, blocking collectives, body(): m = lax.all_to_all(m, 'row', 0, 0, tiled=True).reshape(ROWS * 24, 128)  28.9 us
    pallas_call x4, Pallas kernels, call(): pl.pallas_call(kernel, out_shape=out_shape, in_specs=[spec_s if i < scala...  26.6 us
    ppermute x6, starting transfers between devices, exchange(): lax.ppermute(blocks[d], 'col', [(c, c ^ d) for c in range(COLS)])  11.6 us
    pallas_call x1, Pallas kernels, body(): pl.pallas_call(couple_blocks, out_shape=sds((ROWS, 24, 128), F32), grid_s...  3.19 us
  transfers between devices with their start and end apart: 6, of which 4 were waited for; matrix products, arithmetic and copies ran while one was open for 0% of the time, Pallas kernels for 0%

profile of v4, /device:TPU:1, one launch (start us, length us, event | category | flops | bytes accessed | tf_op | source)
XLA Modules:
  0.0 146.4 jit_solution(179919464353093713)
XLA Ops:
  0.6 0.6 pad_add_fusion.place
  1.3 11.1 %forward_x.1 = (f32[280,384]{1,0:T(8,128)}, f32[280,384]{1,0:T(8,128)}, f32[280,384]{1,0:T(8,128)}, f32[280,384]{1,0:T(8,128)}) custom-call(s32[2]{0:T(128)} %pad_add_fusion.place, s32[4096]{0:T(1024)} %cells.3, f32[4096]{0:T(1024)} %speed.3, f32[384,768]{1,0:T(8,128)} %bitcast.13, f32[384,768]{1,0:T(8,128)} %bitcast.15, f32[384,768]{1,0:T(8,128)} %bitcast.17, ...), custom_call_target="tpu_custom_call" | custom-call | tf_op jit(solution)/shard_map/forward_x/pallas_call | solution.py:506
  12.3 3.3 %collective-permute-start = (f32[280,384]{1,0:T(8,128)}, f32[280,384]{1,0:T(8,128)S(1)}, u32[]{:S(2)}, u32[]{:S(2)}) collective-permute-start(f32[280,384]{1,0:T(8,128)} %get-tuple-element.17), channel_id=1, source_target_pairs={{0,1},{1,0},{2,3},{3,2},{4,5},{5,4},{6,7},{7,6},{8,9},{9,8},{10,11... | collective-permute-start | bytes 1290248 | tf_op jit(solution)/shard_map/ppermute | solution.py:240
  15.6 1.7 %collective-permute-start.2 = (f32[280,384]{1,0:T(8,128)}, f32[280,384]{1,0:T(8,128)S(1)}, u32[]{:S(2)}, u32[]{:S(2)}) collective-permute-start(f32[280,384]{1,0:T(8,128)} %get-tuple-element.19), channel_id=1, source_target_pairs={{0,3},{1,2},{2,1},{3,0},{4,7},{5,6},{6,5},{7,4},{8,11},{9,10},{10,... | collective-permute-start | bytes 1290248 | tf_op jit(solution)/shard_map/ppermute | solution.py:240
  17.4 9.9 %collective-permute-done.1.x2 = f32[280,384]{1,0:T(8,128)S(1)} collective-permute-done((f32[280,384]{1,0:T(8,128)}, f32[280,384]{1,0:T(8,128)S(1)}, u32[]{:S(2)}, u32[]{:S(2)}) %collective-permute-start.1) | collective-permute-done | bytes 430112 | tf_op jit(solution)/shard_map/ppermute | solution.py:240
  27.3 9.4 %collective-permute-done.2.x3 = f32[280,384]{1,0:T(8,128)S(1)} collective-permute-done((f32[280,384]{1,0:T(8,128)}, f32[280,384]{1,0:T(8,128)S(1)}, u32[]{:S(2)}, u32[]{:S(2)}) %collective-permute-start.2) | collective-permute-done | bytes 430112 | tf_op jit(solution)/shard_map/ppermute | solution.py:240
  36.7 1.0 copy-done.4
  37.7 2.8 %forward_z.1 = (f32[1536,128]{1,0:T(8,128)S(1)}, f32[24,3,64,128]{3,2,1,0:T(8,128)S(1)}) custom-call(s32[2]{0:T(128)S(1)} %copy-done.15, f32[280,384]{1,0:T(8,128)S(1)} %copy-done.4, f32[280,384]{1,0:T(8,128)S(1)} %collective-permute-done.x1, f32[280,384]{1,0:T(8,128)S(1)} %collective-permute-done.1.x2, f32[280,384]{1,0:T(8,128)S(1)} %collective-permute-done.2.x3, ...), custom_call_target="tpu_custom_call" | custom-call | tf_op jit(solution)/shard_map/forward_z/pallas_call | solution.py:506
  40.5 35.0 %all_to_all.10.m = f32[64,24,128]{2,1,0:T(8,128)} all-to-all(f32[64,24,128]{2,1,0:T(8,128)S(1)} %bitcast.12), channel_id=1, replica_groups=mesh['row'=64,'col'=4] {'row'}, dimensions={0} | all-to-all | bytes 1572864 | tf_op jit(solution)/shard_map/all_to_all | solution.py:539
  75.5 3.2 %couple_blocks.1 = f32[64,24,128]{2,1,0:T(8,128)} custom-call(s32[2]{0:T(128)} %pad_add_fusion.place, f32[64,24,128]{2,1,0:T(8,128)} %all_to_all.10.m, f32[4,64,2,24,128]{4,3,2,1,0:T(8,128)} %constant.58.clone.cycle), custom_call_target="tpu_custom_call" | custom-call | tf_op jit(solution)/shard_map/couple_blocks/pallas_call | solution.py:540
  78.7 28.9 %all_to_all.11 = f32[64,24,128]{2,1,0:T(8,128)S(1)} all-to-all(f32[64,24,128]{2,1,0:T(8,128)} %couple_blocks.1), channel_id=1, replica_groups=mesh['row'=64,'col'=4] {'row'}, dimensions={0} | all-to-all | bytes 1572864 | tf_op jit(solution)/shard_map/all_to_all | solution.py:551
  107.6 0.0 copy-start
  107.6 0.0 copy-start.1
  107.7 0.0 copy-start.2
  107.7 0.0 copy-start.3
  107.7 0.0 copy-start.8
  107.7 0.0 copy-start.9
  107.7 3.9 %backward_z.1 = (f32[280,384]{1,0:T(8,128)S(1)}, f32[280,384]{1,0:T(8,128)S(1)}, f32[280,384]{1,0:T(8,128)S(1)}, f32[280,384]{1,0:T(8,128)S(1)}) custom-call(s32[2]{0:T(128)S(1)} %copy-done.16, f32[1536,128]{1,0:T(8,128)S(1)} %bitcast.11, f32[24,3,64,128]{3,2,1,0:T(8,128)S(1)} %get-tuple-element.21.keep, bf16[6,224,128]{2,1,0:T(8,128)(2,1)S(1)} %copy-done.12, ...), custom_call_target="tpu_custom_call" | custom-call | tf_op jit(solution)/shard_map/backward_z/pallas_call | solution.py:506
  111.7 4.9 %collective-permute-start.3 = (f32[280,384]{1,0:T(8,128)S(1)}, f32[280,384]{1,0:T(8,128)S(1)}, u32[]{:S(2)}, u32[]{:S(2)}) collective-permute-start(f32[280,384]{1,0:T(8,128)S(1)} %get-tuple-element.23), channel_id=1, source_target_pairs={{0,1},{1,0},{2,3},{3,2},{4,5},{5,4},{6,7},{7,6},{8,9},{9,8},{10,11... | collective-permute-start | bytes 1290248 | tf_op jit(solution)/shard_map/ppermute | solution.py:240
  116.5 0.4 collective-permute-start.4
  116.9 1.3 collective-permute-start.5
  118.3 9.7 %collective-permute-done.4.x2 = f32[280,384]{1,0:T(8,128)S(1)} collective-permute-done((f32[280,384]{1,0:T(8,128)S(1)}, f32[280,384]{1,0:T(8,128)S(1)}, u32[]{:S(2)}, u32[]{:S(2)}) %collective-permute-start.4) | collective-permute-done | bytes 430112 | tf_op jit(solution)/shard_map/ppermute | solution.py:240
  128.0 9.4 %collective-permute-done.5.x3 = f32[280,384]{1,0:T(8,128)S(1)} collective-permute-done((f32[280,384]{1,0:T(8,128)S(1)}, f32[280,384]{1,0:T(8,128)S(1)}, u32[]{:S(2)}, u32[]{:S(2)}) %collective-permute-start.5) | collective-permute-done | bytes 430112 | tf_op jit(solution)/shard_map/ppermute | solution.py:240
  137.5 8.8 %backward_x.1 = (f32[384,768]{1,0:T(8,128)}, f32[384,768]{1,0:T(8,128)}, f32[384,768]{1,0:T(8,128)}) custom-call(s32[2]{0:T(128)S(1)} %copy-done.16, s32[4096]{0:T(1024)S(1)} %copy-done.13, f32[4096]{0:T(1024)S(1)} %copy-done.14, f32[384,768]{1,0:T(8,128)} %bitcast.14, f32[384,768]{1,0:T(8,128)} %bitcast.16, f32[384,768]{1,0:T(8,128)} %bitcast.18, ...), custom_call_target="tpu_custom_call" | custom-call | tf_op jit(solution)/shard_map/backward_x/pallas_call | solution.py:506
  (30 shorter events, 0.1 us)
Async XLA Ops:
  1.2 35.5 %copy-start.5 = (bf16[6,128,224]{2,1,0:T(8,128)(2,1)S(1)}, bf16[6,128,224]{2,1,0:T(8,128)(2,1)}, u32[]{:S(2)}) copy-start(bf16[6,128,224]{2,1,0:T(8,128)(2,1)} %constant.56.clone.wl) | copy-start | bytes 1032196
  1.2 35.5 %copy-start.6 = (bf16[6,128,224]{2,1,0:T(8,128)(2,1)S(1)}, bf16[6,128,224]{2,1,0:T(8,128)(2,1)}, u32[]{:S(2)}) copy-start(bf16[6,128,224]{2,1,0:T(8,128)(2,1)} %constant.55.clone.wh) | copy-start | bytes 1032196
  1.2 35.5 %copy-start.15 = (s32[2]{0:T(128)S(1)}, s32[2]{0:T(128)}, u32[]{:S(2)}) copy-start(s32[2]{0:T(128)} %pad_add_fusion.place) | copy-start | bytes 28
  12.3 5.1 %collective-permute-start = (f32[280,384]{1,0:T(8,128)}, f32[280,384]{1,0:T(8,128)S(1)}, u32[]{:S(2)}, u32[]{:S(2)}) collective-permute-start(f32[280,384]{1,0:T(8,128)} %get-tuple-element.17), channel_id=1, source_target_pairs={{0,1},{1,0},{2,3},{3,2},{4,5},{5,4},{6,7},{7,6},{8,9},{9,8},{10,11... | collective-permute-start | bytes 1290248 | tf_op jit(solution)/shard_map/ppermute | solution.py:240
  15.6 11.7 %collective-permute-start.1 = (f32[280,384]{1,0:T(8,128)}, f32[280,384]{1,0:T(8,128)S(1)}, u32[]{:S(2)}, u32[]{:S(2)}) collective-permute-start(f32[280,384]{1,0:T(8,128)} %get-tuple-element.18), channel_id=1, source_target_pairs={{0,2},{1,3},{2,0},{3,1},{4,6},{5,7},{6,4},{7,5},{8,10},{9,11},{10,... | collective-permute-start | bytes 1290248 | tf_op jit(solution)/shard_map/ppermute | solution.py:240
  15.6 21.1 %collective-permute-start.2 = (f32[280,384]{1,0:T(8,128)}, f32[280,384]{1,0:T(8,128)S(1)}, u32[]{:S(2)}, u32[]{:S(2)}) collective-permute-start(f32[280,384]{1,0:T(8,128)} %get-tuple-element.19), channel_id=1, source_target_pairs={{0,3},{1,2},{2,1},{3,0},{4,7},{5,6},{6,5},{7,4},{8,11},{9,10},{10,... | collective-permute-start | bytes 1290248 | tf_op jit(solution)/shard_map/ppermute | solution.py:240
  36.7 1.0 copy-start.4
  78.7 28.9 %copy-start.11 = (bf16[6,224,128]{2,1,0:T(8,128)(2,1)S(1)}, bf16[6,224,128]{2,1,0:T(8,128)(2,1)}, u32[]{:S(2)}) copy-start(bf16[6,224,128]{2,1,0:T(8,128)(2,1)} %constant.60.clone.wl) | copy-start | bytes 1032196
  78.7 28.9 %copy-start.12 = (bf16[6,224,128]{2,1,0:T(8,128)(2,1)S(1)}, bf16[6,224,128]{2,1,0:T(8,128)(2,1)}, u32[]{:S(2)}) copy-start(bf16[6,224,128]{2,1,0:T(8,128)(2,1)} %constant.59.clone.wh) | copy-start | bytes 1032196
  78.7 28.9 %copy-start.16 = (s32[2]{0:T(128)S(1)}, s32[2]{0:T(128)}, u32[]{:S(2)}) copy-start(s32[2]{0:T(128)} %pad_add_fusion.place) | copy-start | bytes 28
  78.7 58.7 %copy-start.10 = (bf16[384,512]{1,0:T(8,128)(2,1)S(1)}, bf16[384,512]{1,0:T(8,128)(2,1)}, u32[]{:S(2)}) copy-start(bf16[384,512]{1,0:T(8,128)(2,1)} %constant.61.clone.vh) | copy-start | bytes 1179652
  107.6 29.8 %copy-start = (bf16[1280,256]{1,0:T(8,128)(2,1)S(1)}, bf16[1280,256]{1,0:T(8,128)(2,1)}, u32[]{:S(2)}) copy-start(bf16[1280,256]{1,0:T(8,128)(2,1)} %constant.68.clone.dl) | copy-start | bytes 1966084
  107.6 29.7 %copy-start.1 = (bf16[1280,256]{1,0:T(8,128)(2,1)S(1)}, bf16[1280,256]{1,0:T(8,128)(2,1)}, u32[]{:S(2)}) copy-start(bf16[1280,256]{1,0:T(8,128)(2,1)} %constant.67.clone.dh) | copy-start | bytes 1966084
  107.7 29.7 %copy-start.2 = (bf16[1280,256]{1,0:T(8,128)(2,1)S(1)}, bf16[1280,256]{1,0:T(8,128)(2,1)}, u32[]{:S(2)}) copy-start(bf16[1280,256]{1,0:T(8,128)(2,1)} %constant.66.clone.hl) | copy-start | bytes 1966084
  107.7 29.7 %copy-start.3 = (bf16[1280,256]{1,0:T(8,128)(2,1)S(1)}, bf16[1280,256]{1,0:T(8,128)(2,1)}, u32[]{:S(2)}) copy-start(bf16[1280,256]{1,0:T(8,128)(2,1)} %constant.65.clone.hh) | copy-start | bytes 1966084
  107.7 29.7 %copy-start.7 = (bf16[384,432]{1,0:T(8,128)(2,1)S(1)}, bf16[384,432]{1,0:T(8,128)(2,1)}, u32[]{:S(2)}) copy-start(bf16[384,432]{1,0:T(8,128)(2,1)} %constant.64.clone.wl) | copy-start | bytes 995332
  107.7 29.7 %copy-start.8 = (bf16[384,432]{1,0:T(8,128)(2,1)S(1)}, bf16[384,432]{1,0:T(8,128)(2,1)}, u32[]{:S(2)}) copy-start(bf16[384,432]{1,0:T(8,128)(2,1)} %constant.63.clone.wh) | copy-start | bytes 995332
  107.7 29.7 %copy-start.9 = (bf16[384,512]{1,0:T(8,128)(2,1)S(1)}, bf16[384,512]{1,0:T(8,128)(2,1)}, u32[]{:S(2)}) copy-start(bf16[384,512]{1,0:T(8,128)(2,1)} %constant.62.clone.vl) | copy-start | bytes 1179652
  107.7 29.7 %copy-start.13 = (s32[4096]{0:T(1024)S(1)}, s32[4096]{0:T(1024)}, u32[]{:S(2)}) copy-start(s32[4096]{0:T(1024)} %cells.3) | copy-start | bytes 49156
  107.7 29.7 %copy-start.14 = (f32[4096]{0:T(1024)S(1)}, f32[4096]{0:T(1024)}, u32[]{:S(2)}) copy-start(f32[4096]{0:T(1024)} %speed.3) | copy-start | bytes 49156
  111.7 6.6 %collective-permute-start.3 = (f32[280,384]{1,0:T(8,128)S(1)}, f32[280,384]{1,0:T(8,128)S(1)}, u32[]{:S(2)}, u32[]{:S(2)}) collective-permute-start(f32[280,384]{1,0:T(8,128)S(1)} %get-tuple-element.23), channel_id=1, source_target_pairs={{0,1},{1,0},{2,3},{3,2},{4,5},{5,4},{6,7},{7,6},{8,9},{9,8},{10,11... | collective-permute-start | bytes 1290248 | tf_op jit(solution)/shard_map/ppermute | solution.py:240
  116.5 11.5 %collective-permute-start.4 = (f32[280,384]{1,0:T(8,128)S(1)}, f32[280,384]{1,0:T(8,128)S(1)}, u32[]{:S(2)}, u32[]{:S(2)}) collective-permute-start(f32[280,384]{1,0:T(8,128)S(1)} %get-tuple-element.24), channel_id=1, source_target_pairs={{0,2},{1,3},{2,0},{3,1},{4,6},{5,7},{6,4},{7,5},{8,10},{9,11},{10,... | collective-permute-start | bytes 1290248 | tf_op jit(solution)/shard_map/ppermute | solution.py:240
  116.9 20.4 %collective-permute-start.5 = (f32[280,384]{1,0:T(8,128)S(1)}, f32[280,384]{1,0:T(8,128)S(1)}, u32[]{:S(2)}, u32[]{:S(2)}) collective-permute-start(f32[280,384]{1,0:T(8,128)S(1)} %get-tuple-element.25), channel_id=1, source_target_pairs={{0,3},{1,2},{2,1},{3,0},{4,7},{5,6},{6,5},{7,4},{8,11},{9,10},{10,... | collective-permute-start | bytes 1290248 | tf_op jit(solution)/shard_map/ppermute | solution.py:240

commit v5 on v4

--- a/solution.py
+++ b/solution.py
@@ -407,9 +407,12 @@
     return TAIL * RATIO / (1.0 - RATIO * z), TAIL * RATIO / (z - RATIO)
 
 
-def couple_blocks(place, m, cycle, out, hold):
-    ratio = [cycle[0, 0, 0, 8 * t:8 * t + 8, :] for t in range(3)]
-    close = [cycle[0, 0, 1, 8 * t:8 * t + 8, :] for t in range(3)]
+def couple_blocks(place, m, cycle, out, own, hold, sem):
+    copy = pltpu.make_async_copy(cycle.at[place[1], place[0]], own, sem)
+    copy.start()
+    copy.wait()
+    ratio = [own[0, 8 * t:8 * t + 8, :] for t in range(3)]
+    close = [own[1, 8 * t:8 * t + 8, :] for t in range(3)]
     upper = lax.broadcasted_iota(jnp.int32, (8, 128), 0) < 4
 
     def advance(j, s):
@@ -420,7 +423,7 @@
         return tuple(new)
 
     zero = jnp.zeros((8, 128), F32)
-    s = lax.fori_loop(0, ROWS, advance, (zero,) * 3, unroll=4)
+    s = lax.fori_loop(0, ROWS, advance, (zero,) * 3, unroll=8)
     s = tuple(s[t] * close[t] for t in range(3))
 
     def store(j, s):
@@ -428,7 +431,7 @@
             hold[j, 8 * t:8 * t + 8, :] = s[t]
         return advance(j, s)
 
-    lax.fori_loop(0, ROWS, store, s, unroll=4)
+    lax.fori_loop(0, ROWS, store, s, unroll=8)
 
     def merge(j, carry):
         for t in range(3):
@@ -436,7 +439,7 @@
             out[j, rows, :] = jnp.where(upper, hold[j, rows, :], hold[ROWS - 1 - j, rows, :])
         return carry
 
-    lax.fori_loop(0, ROWS, merge, 0, unroll=4)
+    lax.fori_loop(0, ROWS, merge, 0, unroll=8)
 
 
 def backward_z(place, s, keep, wh, wl, o0, o1, o2, o3, out, made):
@@ -537,17 +540,11 @@
         [place, *x, *k["wz"], k["local"]], [pltpu.VMEM(mov, F32), pltpu.SemaphoreType.DMA], 1, anywhere=(7,),
     )
     m = lax.all_to_all(m.reshape(ROWS, 24, 128), "row", 0, 0, tiled=True)
-    m = pl.pallas_call(
-        couple_blocks, out_shape=sds((ROWS, 24, 128), F32),
-        grid_spec=pltpu.PrefetchScalarGridSpec(
-            num_scalar_prefetch=1, grid=(1,),
-            in_specs=[pl.BlockSpec((ROWS, 24, 128), lambda i, p: (0, 0, 0)),
-                      pl.BlockSpec((1, 1, 2, 24, 128), lambda i, p: (p[1], p[0], 0, 0, 0))],
-            out_specs=pl.BlockSpec((ROWS, 24, 128), lambda i, p: (0, 0, 0)),
-            scratch_shapes=[pltpu.VMEM((ROWS, 24, 128), F32)],
-        ),
-        name="couple_blocks",
-    )(place, m, k["cycle"])
+    m = call(
+        couple_blocks, sds((ROWS, 24, 128), F32), [place, m, k["cycle"]],
+        [pltpu.VMEM((2, 24, 128), F32), pltpu.VMEM((ROWS, 24, 128), F32), pltpu.SemaphoreType.DMA],
+        1, anywhere=(2,), vmem=16,
+    )
     m = lax.all_to_all(m, "row", 0, 0, tiled=True).reshape(ROWS * 24, 128)
     x = call(
         backward_z, [sds(mov[1:], F32)] * COLS, [place, m, keep, *k["wz_t"]],

time: 147 us -> 145 us (0.986)
  Pallas kernels: 29.7 us -> 27.9 us
    pallas_call x1 -> x0, Pallas kernels: 3.19 us -> none  [body(): pl.pallas_call(couple_blocks, out_shape=sds((ROWS, 24, 128), F32), grid_s...]
    pallas_call x4 -> x5, Pallas kernels: 26.6 us -> 27.9 us  [call(): pl.pallas_call(kernel, out_shape=out_shape, in_specs=[spec_s if i < scala...]
where the time goes in v5:
time: 145 us; the launch traced here: 144 us
  blocking collectives  63.6 us (44%)
  waiting for transfers between devices  38.5 us (27%)
  Pallas kernels  27.9 us (19%)
  starting transfers between devices  11.7 us (8%)
    ppermute x6, waiting for transfers between devices, exchange(): lax.ppermute(blocks[d], 'col', [(c, c ^ d) for c in range(COLS)])  38.5 us
    all_to_all x1, blocking collectives, body(): m = lax.all_to_all(m.reshape(ROWS, 24, 128), 'row', 0, 0, tiled=True)  34.9 us
    all_to_all x1, blocking collectives, body(): m = lax.all_to_all(m, 'row', 0, 0, tiled=True).reshape(ROWS * 24, 128)  28.7 us
    pallas_call x5, Pallas kernels, call(): pl.pallas_call(kernel, out_shape=out_shape, in_specs=[spec_s if i < scala...  27.9 us
    ppermute x6, starting transfers between devices, exchange(): lax.ppermute(blocks[d], 'col', [(c, c ^ d) for c in range(COLS)])  11.7 us
  transfers between devices with their start and end apart: 6, of which 4 were waited for; matrix products, arithmetic and copies ran while one was open for 0% of the time, Pallas kernels for 0%

profile of v5, /device:TPU:1, one launch (start us, length us, event | category | flops | bytes accessed | tf_op | source)
XLA Modules:
  0.0 144.3 jit_solution(12397373434560131325)
XLA Ops:
  0.6 0.6 pad_add_fusion.place
  1.2 11.1 %forward_x.1 = (f32[280,384]{1,0:T(8,128)}, f32[280,384]{1,0:T(8,128)}, f32[280,384]{1,0:T(8,128)}, f32[280,384]{1,0:T(8,128)}) custom-call(s32[2]{0:T(128)} %pad_add_fusion.place, s32[4096]{0:T(1024)} %cells.3, f32[4096]{0:T(1024)} %speed.3, f32[384,768]{1,0:T(8,128)} %bitcast.13, f32[384,768]{1,0:T(8,128)} %bitcast.15, f32[384,768]{1,0:T(8,128)} %bitcast.17, ...), custom_call_target="tpu_custom_call" | custom-call | tf_op jit(solution)/shard_map/forward_x/pallas_call | solution.py:509
  12.3 3.3 %collective-permute-start = (f32[280,384]{1,0:T(8,128)}, f32[280,384]{1,0:T(8,128)S(1)}, u32[]{:S(2)}, u32[]{:S(2)}) collective-permute-start(f32[280,384]{1,0:T(8,128)} %get-tuple-element.17), channel_id=1, source_target_pairs={{0,1},{1,0},{2,3},{3,2},{4,5},{5,4},{6,7},{7,6},{8,9},{9,8},{10,11... | collective-permute-start | bytes 1290248 | tf_op jit(solution)/shard_map/ppermute | solution.py:240
  15.6 1.7 %collective-permute-start.2 = (f32[280,384]{1,0:T(8,128)}, f32[280,384]{1,0:T(8,128)S(1)}, u32[]{:S(2)}, u32[]{:S(2)}) collective-permute-start(f32[280,384]{1,0:T(8,128)} %get-tuple-element.19), channel_id=1, source_target_pairs={{0,3},{1,2},{2,1},{3,0},{4,7},{5,6},{6,5},{7,4},{8,11},{9,10},{10,... | collective-permute-start | bytes 1290248 | tf_op jit(solution)/shard_map/ppermute | solution.py:240
  17.4 9.9 %collective-permute-done.1.x2 = f32[280,384]{1,0:T(8,128)S(1)} collective-permute-done((f32[280,384]{1,0:T(8,128)}, f32[280,384]{1,0:T(8,128)S(1)}, u32[]{:S(2)}, u32[]{:S(2)}) %collective-permute-start.1) | collective-permute-done | bytes 430112 | tf_op jit(solution)/shard_map/ppermute | solution.py:240
  27.3 9.4 %collective-permute-done.2.x3 = f32[280,384]{1,0:T(8,128)S(1)} collective-permute-done((f32[280,384]{1,0:T(8,128)}, f32[280,384]{1,0:T(8,128)S(1)}, u32[]{:S(2)}, u32[]{:S(2)}) %collective-permute-start.2) | collective-permute-done | bytes 430112 | tf_op jit(solution)/shard_map/ppermute | solution.py:240
  36.7 1.0 copy-done.5
  37.7 3.1 %forward_z.1 = (f32[1536,128]{1,0:T(8,128)S(1)}, f32[24,3,64,128]{3,2,1,0:T(8,128)S(1)}) custom-call(s32[2]{0:T(128)S(1)} %copy-done.16, f32[280,384]{1,0:T(8,128)S(1)} %copy-done.5, f32[280,384]{1,0:T(8,128)S(1)} %collective-permute-done.x1, f32[280,384]{1,0:T(8,128)S(1)} %collective-permute-done.1.x2, f32[280,384]{1,0:T(8,128)S(1)} %collective-permute-done.2.x3, ...), custom_call_target="tpu_custom_call" | custom-call | tf_op jit(solution)/shard_map/forward_z/pallas_call | solution.py:509
  40.8 34.9 %all_to_all.10.m = f32[64,24,128]{2,1,0:T(8,128)S(1)} all-to-all(f32[64,24,128]{2,1,0:T(8,128)S(1)} %bitcast.12), channel_id=1, replica_groups=mesh['row'=64,'col'=4] {'row'}, dimensions={0} | all-to-all | bytes 1572864 | tf_op jit(solution)/shard_map/all_to_all | solution.py:542
  75.7 1.0 couple_blocks.1
  76.7 0.0 copy-start.12
  76.7 0.0 copy-start.13
  76.7 0.0 copy-start.11
  76.7 28.7 %all_to_all.11 = f32[64,24,128]{2,1,0:T(8,128)S(1)} all-to-all(f32[64,24,128]{2,1,0:T(8,128)S(1)} %couple_blocks.1), channel_id=1, replica_groups=mesh['row'=64,'col'=4] {'row'}, dimensions={0} | all-to-all | bytes 1572864 | tf_op jit(solution)/shard_map/all_to_all | solution.py:548
  105.4 0.0 copy-start.3
  105.5 0.0 copy-start.8
  105.5 0.0 copy-start.9
  105.5 3.9 %backward_z.1 = (f32[280,384]{1,0:T(8,128)S(1)}, f32[280,384]{1,0:T(8,128)S(1)}, f32[280,384]{1,0:T(8,128)S(1)}, f32[280,384]{1,0:T(8,128)S(1)}) custom-call(s32[2]{0:T(128)S(1)} %copy-done.16, f32[1536,128]{1,0:T(8,128)S(1)} %bitcast.11, f32[24,3,64,128]{3,2,1,0:T(8,128)S(1)} %get-tuple-element.21.keep, bf16[6,224,128]{2,1,0:T(8,128)(2,1)S(1)} %copy-done.13, ...), custom_call_target="tpu_custom_call" | custom-call | tf_op jit(solution)/shard_map/backward_z/pallas_call | solution.py:509
  109.4 4.9 %collective-permute-start.3 = (f32[280,384]{1,0:T(8,128)S(1)}, f32[280,384]{1,0:T(8,128)S(1)}, u32[]{:S(2)}, u32[]{:S(2)}) collective-permute-start(f32[280,384]{1,0:T(8,128)S(1)} %get-tuple-element.23), channel_id=1, source_target_pairs={{0,1},{1,0},{2,3},{3,2},{4,5},{5,4},{6,7},{7,6},{8,9},{9,8},{10,11... | collective-permute-start | bytes 1290248 | tf_op jit(solution)/shard_map/ppermute | solution.py:240
  114.3 0.4 collective-permute-start.4
  114.7 1.3 collective-permute-start.5
  116.0 9.7 %collective-permute-done.4.x2 = f32[280,384]{1,0:T(8,128)S(1)} collective-permute-done((f32[280,384]{1,0:T(8,128)S(1)}, f32[280,384]{1,0:T(8,128)S(1)}, u32[]{:S(2)}, u32[]{:S(2)}) %collective-permute-start.4) | collective-permute-done | bytes 430112 | tf_op jit(solution)/shard_map/ppermute | solution.py:240
  125.8 9.4 %collective-permute-done.5.x3 = f32[280,384]{1,0:T(8,128)S(1)} collective-permute-done((f32[280,384]{1,0:T(8,128)S(1)}, f32[280,384]{1,0:T(8,128)S(1)}, u32[]{:S(2)}, u32[]{:S(2)}) %collective-permute-start.5) | collective-permute-done | bytes 430112 | tf_op jit(solution)/shard_map/ppermute | solution.py:240
  135.2 8.9 %backward_x.1 = (f32[384,768]{1,0:T(8,128)}, f32[384,768]{1,0:T(8,128)}, f32[384,768]{1,0:T(8,128)}) custom-call(s32[2]{0:T(128)S(1)} %copy-done.16, s32[4096]{0:T(1024)S(1)} %copy-done.14, f32[4096]{0:T(1024)S(1)} %copy-done.15, f32[384,768]{1,0:T(8,128)} %bitcast.14, f32[384,768]{1,0:T(8,128)} %bitcast.16, f32[384,768]{1,0:T(8,128)} %bitcast.18, ...), custom_call_target="tpu_custom_call" | custom-call | tf_op jit(solution)/shard_map/backward_x/pallas_call | solution.py:509
  (30 shorter events, 0.1 us)
Async XLA Ops:
  1.2 35.5 %copy-start.6 = (bf16[6,128,224]{2,1,0:T(8,128)(2,1)S(1)}, bf16[6,128,224]{2,1,0:T(8,128)(2,1)}, u32[]{:S(2)}) copy-start(bf16[6,128,224]{2,1,0:T(8,128)(2,1)} %constant.56.clone.wl) | copy-start | bytes 1032196
  1.2 35.5 %copy-start.7 = (bf16[6,128,224]{2,1,0:T(8,128)(2,1)S(1)}, bf16[6,128,224]{2,1,0:T(8,128)(2,1)}, u32[]{:S(2)}) copy-start(bf16[6,128,224]{2,1,0:T(8,128)(2,1)} %constant.55.clone.wh) | copy-start | bytes 1032196
  1.2 35.5 %copy-start.16 = (s32[2]{0:T(128)S(1)}, s32[2]{0:T(128)}, u32[]{:S(2)}) copy-start(s32[2]{0:T(128)} %pad_add_fusion.place) | copy-start | bytes 28
  12.3 5.1 %collective-permute-start = (f32[280,384]{1,0:T(8,128)}, f32[280,384]{1,0:T(8,128)S(1)}, u32[]{:S(2)}, u32[]{:S(2)}) collective-permute-start(f32[280,384]{1,0:T(8,128)} %get-tuple-element.17), channel_id=1, source_target_pairs={{0,1},{1,0},{2,3},{3,2},{4,5},{5,4},{6,7},{7,6},{8,9},{9,8},{10,11... | collective-permute-start | bytes 1290248 | tf_op jit(solution)/shard_map/ppermute | solution.py:240
  15.6 11.7 %collective-permute-start.1 = (f32[280,384]{1,0:T(8,128)}, f32[280,384]{1,0:T(8,128)S(1)}, u32[]{:S(2)}, u32[]{:S(2)}) collective-permute-start(f32[280,384]{1,0:T(8,128)} %get-tuple-element.18), channel_id=1, source_target_pairs={{0,2},{1,3},{2,0},{3,1},{4,6},{5,7},{6,4},{7,5},{8,10},{9,11},{10,... | collective-permute-start | bytes 1290248 | tf_op jit(solution)/shard_map/ppermute | solution.py:240
  15.6 21.1 %collective-permute-start.2 = (f32[280,384]{1,0:T(8,128)}, f32[280,384]{1,0:T(8,128)S(1)}, u32[]{:S(2)}, u32[]{:S(2)}) collective-permute-start(f32[280,384]{1,0:T(8,128)} %get-tuple-element.19), channel_id=1, source_target_pairs={{0,3},{1,2},{2,1},{3,0},{4,7},{5,6},{6,5},{7,4},{8,11},{9,10},{10,... | collective-permute-start | bytes 1290248 | tf_op jit(solution)/shard_map/ppermute | solution.py:240
  36.7 1.0 copy-start.5
  37.7 38.0 %copy-start = (f32[4,64,2,24,128]{4,3,2,1,0:T(8,128)S(1)}, f32[4,64,2,24,128]{4,3,2,1,0:T(8,128)}, u32[]{:S(2)}) copy-start(f32[4,64,2,24,128]{4,3,2,1,0:T(8,128)} %constant.58.clone.cycle) | copy-start | bytes 18874372
  76.7 28.7 %copy-start.12 = (bf16[6,224,128]{2,1,0:T(8,128)(2,1)S(1)}, bf16[6,224,128]{2,1,0:T(8,128)(2,1)}, u32[]{:S(2)}) copy-start(bf16[6,224,128]{2,1,0:T(8,128)(2,1)} %constant.60.clone.wl) | copy-start | bytes 1032196
  76.7 28.7 %copy-start.13 = (bf16[6,224,128]{2,1,0:T(8,128)(2,1)S(1)}, bf16[6,224,128]{2,1,0:T(8,128)(2,1)}, u32[]{:S(2)}) copy-start(bf16[6,224,128]{2,1,0:T(8,128)(2,1)} %constant.59.clone.wh) | copy-start | bytes 1032196
  76.7 58.4 %copy-start.11 = (bf16[384,512]{1,0:T(8,128)(2,1)S(1)}, bf16[384,512]{1,0:T(8,128)(2,1)}, u32[]{:S(2)}) copy-start(bf16[384,512]{1,0:T(8,128)(2,1)} %constant.61.clone.vh) | copy-start | bytes 1179652
  105.4 29.7 %copy-start.1 = (bf16[1280,256]{1,0:T(8,128)(2,1)S(1)}, bf16[1280,256]{1,0:T(8,128)(2,1)}, u32[]{:S(2)}) copy-start(bf16[1280,256]{1,0:T(8,128)(2,1)} %constant.68.clone.dl) | copy-start | bytes 1966084
  105.4 29.7 %copy-start.2 = (bf16[1280,256]{1,0:T(8,128)(2,1)S(1)}, bf16[1280,256]{1,0:T(8,128)(2,1)}, u32[]{:S(2)}) copy-start(bf16[1280,256]{1,0:T(8,128)(2,1)} %constant.67.clone.dh) | copy-start | bytes 1966084
  105.4 29.7 %copy-start.3 = (bf16[1280,256]{1,0:T(8,128)(2,1)S(1)}, bf16[1280,256]{1,0:T(8,128)(2,1)}, u32[]{:S(2)}) copy-start(bf16[1280,256]{1,0:T(8,128)(2,1)} %constant.66.clone.hl) | copy-start | bytes 1966084
  105.4 29.7 %copy-start.4 = (bf16[1280,256]{1,0:T(8,128)(2,1)S(1)}, bf16[1280,256]{1,0:T(8,128)(2,1)}, u32[]{:S(2)}) copy-start(bf16[1280,256]{1,0:T(8,128)(2,1)} %constant.65.clone.hh) | copy-start | bytes 1966084
  105.5 29.7 %copy-start.8 = (bf16[384,432]{1,0:T(8,128)(2,1)S(1)}, bf16[384,432]{1,0:T(8,128)(2,1)}, u32[]{:S(2)}) copy-start(bf16[384,432]{1,0:T(8,128)(2,1)} %constant.64.clone.wl) | copy-start | bytes 995332
  105.5 29.7 %copy-start.9 = (bf16[384,432]{1,0:T(8,128)(2,1)S(1)}, bf16[384,432]{1,0:T(8,128)(2,1)}, u32[]{:S(2)}) copy-start(bf16[384,432]{1,0:T(8,128)(2,1)} %constant.63.clone.wh) | copy-start | bytes 995332
  105.5 29.7 %copy-start.10 = (bf16[384,512]{1,0:T(8,128)(2,1)S(1)}, bf16[384,512]{1,0:T(8,128)(2,1)}, u32[]{:S(2)}) copy-start(bf16[384,512]{1,0:T(8,128)(2,1)} %constant.62.clone.vl) | copy-start | bytes 1179652
  105.5 29.7 %copy-start.14 = (s32[4096]{0:T(1024)S(1)}, s32[4096]{0:T(1024)}, u32[]{:S(2)}) copy-start(s32[4096]{0:T(1024)} %cells.3) | copy-start | bytes 49156
  105.5 29.7 %copy-start.15 = (f32[4096]{0:T(1024)S(1)}, f32[4096]{0:T(1024)}, u32[]{:S(2)}) copy-start(f32[4096]{0:T(1024)} %speed.3) | copy-start | bytes 49156
  109.4 6.6 %collective-permute-start.3 = (f32[280,384]{1,0:T(8,128)S(1)}, f32[280,384]{1,0:T(8,128)S(1)}, u32[]{:S(2)}, u32[]{:S(2)}) collective-permute-start(f32[280,384]{1,0:T(8,128)S(1)} %get-tuple-element.23), channel_id=1, source_target_pairs={{0,1},{1,0},{2,3},{3,2},{4,5},{5,4},{6,7},{7,6},{8,9},{9,8},{10,11... | collective-permute-start | bytes 1290248 | tf_op jit(solution)/shard_map/ppermute | solution.py:240
  114.3 11.5 %collective-permute-start.4 = (f32[280,384]{1,0:T(8,128)S(1)}, f32[280,384]{1,0:T(8,128)S(1)}, u32[]{:S(2)}, u32[]{:S(2)}) collective-permute-start(f32[280,384]{1,0:T(8,128)S(1)} %get-tuple-element.24), channel_id=1, source_target_pairs={{0,2},{1,3},{2,0},{3,1},{4,6},{5,7},{6,4},{7,5},{8,10},{9,11},{10,... | collective-permute-start | bytes 1290248 | tf_op jit(solution)/shard_map/ppermute | solution.py:240
  114.7 20.4 %collective-permute-start.5 = (f32[280,384]{1,0:T(8,128)S(1)}, f32[280,384]{1,0:T(8,128)S(1)}, u32[]{:S(2)}, u32[]{:S(2)}) collective-permute-start(f32[280,384]{1,0:T(8,128)S(1)} %get-tuple-element.25), channel_id=1, source_target_pairs={{0,3},{1,2},{2,1},{3,0},{4,7},{5,6},{6,5},{7,4},{8,11},{9,10},{10,... | collective-permute-start | bytes 1290248 | tf_op jit(solution)/shard_map/ppermute | solution.py:240

commit v6 on v5

--- a/solution.py
+++ b/solution.py
@@ -285,7 +285,14 @@
                 c = 2 * (c - 4)
                 out[c, :, 256:384] = join(a, b)
                 out[c + 1, :, 256:384] = join_high(a, b)
-    deal(place, out, (o0, o1, o2, o3))
+    copies = [
+        pltpu.make_async_copy(out.at[place[1] ^ d], target, sems.at[10 + d])
+        for d, target in enumerate((o0, o1, o2, o3))
+    ]
+    for copy in copies:
+        copy.start()
+    for copy in copies:
+        copy.wait()
 
 
 def backward_x(place, cells, speed, u, v, w, solid, x0, x1, x2, x3, vh, vl, wh, wl, hh, hl, dh, dl,
@@ -532,7 +539,7 @@
         forward_x, [sds(mov[1:], F32)] * COLS,
         [place, inflow_cells, inflow_speed, *fields, *k["left"], *k["hx"], *k["fwd_dx"]],
         [pltpu.VMEM(mov, F32)] + [pltpu.VMEM(flat, F32)] * 3 + [pltpu.VMEM(flat, jnp.int32)] + [pltpu.VMEM((560, NX), BF16)] * 2
-        + [pltpu.VMEM((1280, 256), BF16)] * 4 + [pltpu.SemaphoreType.DMA((10,))], 3, range(3, 13), vmem=60,
+        + [pltpu.VMEM((1280, 256), BF16)] * 4 + [pltpu.SemaphoreType.DMA((14,))], 3, range(3, 13), out_space=pltpu.HBM, vmem=60,
     )
     x = exchange(x)
     m, keep = call(

time: 145 us -> 145 us (level)
  no operation moved by 1% of the time
where the time goes in v6:
time: 145 us; the launch traced here: 144 us
  blocking collectives  63.6 us (44%)
  waiting for transfers between devices  38.5 us (27%)
  Pallas kernels  27.9 us (19%)
  starting transfers between devices  11.6 us (8%)
    ppermute x6, waiting for transfers between devices, exchange(): lax.ppermute(blocks[d], 'col', [(c, c ^ d) for c in range(COLS)])  38.5 us
    all_to_all x1, blocking collectives, body(): m = lax.all_to_all(m.reshape(ROWS, 24, 128), 'row', 0, 0, tiled=True)  34.9 us
    all_to_all x1, blocking collectives, body(): m = lax.all_to_all(m, 'row', 0, 0, tiled=True).reshape(ROWS * 24, 128)  28.7 us
    pallas_call x5, Pallas kernels, call(): pl.pallas_call(kernel, out_shape=out_shape, in_specs=[spec_s if i < scala...  27.9 us
    ppermute x6, starting transfers between devices, exchange(): lax.ppermute(blocks[d], 'col', [(c, c ^ d) for c in range(COLS)])  11.6 us
  transfers between devices with their start and end apart: 6, of which 4 were waited for; matrix products, arithmetic and copies ran while one was open for 0% of the time, Pallas kernels for 0%

profile of v6, /device:TPU:1, one launch (start us, length us, event | category | flops | bytes accessed | tf_op | source)
XLA Modules:
  0.0 144.3 jit_solution(9482064869431087129)
XLA Ops:
  0.6 0.6 pad_add_fusion.place
  1.2 11.1 %forward_x.1 = (f32[280,384]{1,0:T(8,128)}, f32[280,384]{1,0:T(8,128)}, f32[280,384]{1,0:T(8,128)}, f32[280,384]{1,0:T(8,128)}) custom-call(s32[2]{0:T(128)} %pad_add_fusion.place, s32[4096]{0:T(1024)} %cells.3, f32[4096]{0:T(1024)} %speed.3, f32[384,768]{1,0:T(8,128)} %bitcast.13, f32[384,768]{1,0:T(8,128)} %bitcast.15, f32[384,768]{1,0:T(8,128)} %bitcast.17, ...), custom_call_target="tpu_custom_call" | custom-call | tf_op jit(solution)/shard_map/forward_x/pallas_call | solution.py:516
  12.3 3.3 %collective-permute-start = (f32[280,384]{1,0:T(8,128)}, f32[280,384]{1,0:T(8,128)S(1)}, u32[]{:S(2)}, u32[]{:S(2)}) collective-permute-start(f32[280,384]{1,0:T(8,128)} %get-tuple-element.17), channel_id=1, source_target_pairs={{0,1},{1,0},{2,3},{3,2},{4,5},{5,4},{6,7},{7,6},{8,9},{9,8},{10,11... | collective-permute-start | bytes 1290248 | tf_op jit(solution)/shard_map/ppermute | solution.py:240
  15.6 1.7 %collective-permute-start.2 = (f32[280,384]{1,0:T(8,128)}, f32[280,384]{1,0:T(8,128)S(1)}, u32[]{:S(2)}, u32[]{:S(2)}) collective-permute-start(f32[280,384]{1,0:T(8,128)} %get-tuple-element.19), channel_id=1, source_target_pairs={{0,3},{1,2},{2,1},{3,0},{4,7},{5,6},{6,5},{7,4},{8,11},{9,10},{10,... | collective-permute-start | bytes 1290248 | tf_op jit(solution)/shard_map/ppermute | solution.py:240
  17.3 9.9 %collective-permute-done.1.x2 = f32[280,384]{1,0:T(8,128)S(1)} collective-permute-done((f32[280,384]{1,0:T(8,128)}, f32[280,384]{1,0:T(8,128)S(1)}, u32[]{:S(2)}, u32[]{:S(2)}) %collective-permute-start.1) | collective-permute-done | bytes 430112 | tf_op jit(solution)/shard_map/ppermute | solution.py:240
  27.3 9.4 %collective-permute-done.2.x3 = f32[280,384]{1,0:T(8,128)S(1)} collective-permute-done((f32[280,384]{1,0:T(8,128)}, f32[280,384]{1,0:T(8,128)S(1)}, u32[]{:S(2)}, u32[]{:S(2)}) %collective-permute-start.2) | collective-permute-done | bytes 430112 | tf_op jit(solution)/shard_map/ppermute | solution.py:240
  36.7 1.0 copy-done.5
  37.7 3.1 %forward_z.1 = (f32[1536,128]{1,0:T(8,128)S(1)}, f32[24,3,64,128]{3,2,1,0:T(8,128)S(1)}) custom-call(s32[2]{0:T(128)S(1)} %copy-done.16, f32[280,384]{1,0:T(8,128)S(1)} %copy-done.5, f32[280,384]{1,0:T(8,128)S(1)} %collective-permute-done.x1, f32[280,384]{1,0:T(8,128)S(1)} %collective-permute-done.1.x2, f32[280,384]{1,0:T(8,128)S(1)} %collective-permute-done.2.x3, ...), custom_call_target="tpu_custom_call" | custom-call | tf_op jit(solution)/shard_map/forward_z/pallas_call | solution.py:516
  40.8 34.9 %all_to_all.10.m = f32[64,24,128]{2,1,0:T(8,128)S(1)} all-to-all(f32[64,24,128]{2,1,0:T(8,128)S(1)} %bitcast.12), channel_id=1, replica_groups=mesh['row'=64,'col'=4] {'row'}, dimensions={0} | all-to-all | bytes 1572864 | tf_op jit(solution)/shard_map/all_to_all | solution.py:549
  75.7 1.0 couple_blocks.1
  76.7 0.0 copy-start.12
  76.7 0.0 copy-start.13
  76.7 0.0 copy-start.11
  76.7 28.7 %all_to_all.11 = f32[64,24,128]{2,1,0:T(8,128)S(1)} all-to-all(f32[64,24,128]{2,1,0:T(8,128)S(1)} %couple_blocks.1), channel_id=1, replica_groups=mesh['row'=64,'col'=4] {'row'}, dimensions={0} | all-to-all | bytes 1572864 | tf_op jit(solution)/shard_map/all_to_all | solution.py:555
  105.4 0.0 copy-start.3
  105.4 0.0 copy-start.4
  105.5 0.0 copy-start.8
  105.5 3.9 %backward_z.1 = (f32[280,384]{1,0:T(8,128)S(1)}, f32[280,384]{1,0:T(8,128)S(1)}, f32[280,384]{1,0:T(8,128)S(1)}, f32[280,384]{1,0:T(8,128)S(1)}) custom-call(s32[2]{0:T(128)S(1)} %copy-done.16, f32[1536,128]{1,0:T(8,128)S(1)} %bitcast.11, f32[24,3,64,128]{3,2,1,0:T(8,128)S(1)} %get-tuple-element.21.keep, bf16[6,224,128]{2,1,0:T(8,128)(2,1)S(1)} %copy-done.13, ...), custom_call_target="tpu_custom_call" | custom-call | tf_op jit(solution)/shard_map/backward_z/pallas_call | solution.py:516
  109.4 4.9 %collective-permute-start.3 = (f32[280,384]{1,0:T(8,128)S(1)}, f32[280,384]{1,0:T(8,128)S(1)}, u32[]{:S(2)}, u32[]{:S(2)}) collective-permute-start(f32[280,384]{1,0:T(8,128)S(1)} %get-tuple-element.23), channel_id=1, source_target_pairs={{0,1},{1,0},{2,3},{3,2},{4,5},{5,4},{6,7},{7,6},{8,9},{9,8},{10,11... | collective-permute-start | bytes 1290248 | tf_op jit(solution)/shard_map/ppermute | solution.py:240
  114.3 0.4 collective-permute-start.4
  114.7 1.3 collective-permute-start.5
  116.0 9.7 %collective-permute-done.4.x2 = f32[280,384]{1,0:T(8,128)S(1)} collective-permute-done((f32[280,384]{1,0:T(8,128)S(1)}, f32[280,384]{1,0:T(8,128)S(1)}, u32[]{:S(2)}, u32[]{:S(2)}) %collective-permute-start.4) | collective-permute-done | bytes 430112 | tf_op jit(solution)/shard_map/ppermute | solution.py:240
  125.8 9.4 %collective-permute-done.5.x3 = f32[280,384]{1,0:T(8,128)S(1)} collective-permute-done((f32[280,384]{1,0:T(8,128)S(1)}, f32[280,384]{1,0:T(8,128)S(1)}, u32[]{:S(2)}, u32[]{:S(2)}) %collective-permute-start.5) | collective-permute-done | bytes 430112 | tf_op jit(solution)/shard_map/ppermute | solution.py:240
  135.2 8.9 %backward_x.1 = (f32[384,768]{1,0:T(8,128)}, f32[384,768]{1,0:T(8,128)}, f32[384,768]{1,0:T(8,128)}) custom-call(s32[2]{0:T(128)S(1)} %copy-done.16, s32[4096]{0:T(1024)S(1)} %copy-done.14, f32[4096]{0:T(1024)S(1)} %copy-done.15, f32[384,768]{1,0:T(8,128)} %bitcast.14, f32[384,768]{1,0:T(8,128)} %bitcast.16, f32[384,768]{1,0:T(8,128)} %bitcast.18, ...), custom_call_target="tpu_custom_call" | custom-call | tf_op jit(solution)/shard_map/backward_x/pallas_call | solution.py:516
  (30 shorter events, 0.1 us)
Async XLA Ops:
  1.2 35.5 %copy-start.6 = (bf16[6,128,224]{2,1,0:T(8,128)(2,1)S(1)}, bf16[6,128,224]{2,1,0:T(8,128)(2,1)}, u32[]{:S(2)}) copy-start(bf16[6,128,224]{2,1,0:T(8,128)(2,1)} %constant.56.clone.wl) | copy-start | bytes 1032196
  1.2 35.5 %copy-start.7 = (bf16[6,128,224]{2,1,0:T(8,128)(2,1)S(1)}, bf16[6,128,224]{2,1,0:T(8,128)(2,1)}, u32[]{:S(2)}) copy-start(bf16[6,128,224]{2,1,0:T(8,128)(2,1)} %constant.55.clone.wh) | copy-start | bytes 1032196
  1.2 35.5 %copy-start.16 = (s32[2]{0:T(128)S(1)}, s32[2]{0:T(128)}, u32[]{:S(2)}) copy-start(s32[2]{0:T(128)} %pad_add_fusion.place) | copy-start | bytes 28
  12.3 5.1 %collective-permute-start = (f32[280,384]{1,0:T(8,128)}, f32[280,384]{1,0:T(8,128)S(1)}, u32[]{:S(2)}, u32[]{:S(2)}) collective-permute-start(f32[280,384]{1,0:T(8,128)} %get-tuple-element.17), channel_id=1, source_target_pairs={{0,1},{1,0},{2,3},{3,2},{4,5},{5,4},{6,7},{7,6},{8,9},{9,8},{10,11... | collective-permute-start | bytes 1290248 | tf_op jit(solution)/shard_map/ppermute | solution.py:240
  15.6 11.7 %collective-permute-start.1 = (f32[280,384]{1,0:T(8,128)}, f32[280,384]{1,0:T(8,128)S(1)}, u32[]{:S(2)}, u32[]{:S(2)}) collective-permute-start(f32[280,384]{1,0:T(8,128)} %get-tuple-element.18), channel_id=1, source_target_pairs={{0,2},{1,3},{2,0},{3,1},{4,6},{5,7},{6,4},{7,5},{8,10},{9,11},{10,... | collective-permute-start | bytes 1290248 | tf_op jit(solution)/shard_map/ppermute | solution.py:240
  15.6 21.1 %collective-permute-start.2 = (f32[280,384]{1,0:T(8,128)}, f32[280,384]{1,0:T(8,128)S(1)}, u32[]{:S(2)}, u32[]{:S(2)}) collective-permute-start(f32[280,384]{1,0:T(8,128)} %get-tuple-element.19), channel_id=1, source_target_pairs={{0,3},{1,2},{2,1},{3,0},{4,7},{5,6},{6,5},{7,4},{8,11},{9,10},{10,... | collective-permute-start | bytes 1290248 | tf_op jit(solution)/shard_map/ppermute | solution.py:240
  36.7 1.0 copy-start.5
  37.7 38.0 %copy-start = (f32[4,64,2,24,128]{4,3,2,1,0:T(8,128)S(1)}, f32[4,64,2,24,128]{4,3,2,1,0:T(8,128)}, u32[]{:S(2)}) copy-start(f32[4,64,2,24,128]{4,3,2,1,0:T(8,128)} %constant.58.clone.cycle) | copy-start | bytes 18874372
  76.7 28.7 %copy-start.12 = (bf16[6,224,128]{2,1,0:T(8,128)(2,1)S(1)}, bf16[6,224,128]{2,1,0:T(8,128)(2,1)}, u32[]{:S(2)}) copy-start(bf16[6,224,128]{2,1,0:T(8,128)(2,1)} %constant.60.clone.wl) | copy-start | bytes 1032196
  76.7 28.7 %copy-start.13 = (bf16[6,224,128]{2,1,0:T(8,128)(2,1)S(1)}, bf16[6,224,128]{2,1,0:T(8,128)(2,1)}, u32[]{:S(2)}) copy-start(bf16[6,224,128]{2,1,0:T(8,128)(2,1)} %constant.59.clone.wh) | copy-start | bytes 1032196
  76.7 58.4 %copy-start.11 = (bf16[384,512]{1,0:T(8,128)(2,1)S(1)}, bf16[384,512]{1,0:T(8,128)(2,1)}, u32[]{:S(2)}) copy-start(bf16[384,512]{1,0:T(8,128)(2,1)} %constant.61.clone.vh) | copy-start | bytes 1179652
  105.4 29.7 %copy-start.1 = (bf16[1280,256]{1,0:T(8,128)(2,1)S(1)}, bf16[1280,256]{1,0:T(8,128)(2,1)}, u32[]{:S(2)}) copy-start(bf16[1280,256]{1,0:T(8,128)(2,1)} %constant.68.clone.dl) | copy-start | bytes 1966084
  105.4 29.7 %copy-start.2 = (bf16[1280,256]{1,0:T(8,128)(2,1)S(1)}, bf16[1280,256]{1,0:T(8,128)(2,1)}, u32[]{:S(2)}) copy-start(bf16[1280,256]{1,0:T(8,128)(2,1)} %constant.67.clone.dh) | copy-start | bytes 1966084
  105.4 29.7 %copy-start.3 = (bf16[1280,256]{1,0:T(8,128)(2,1)S(1)}, bf16[1280,256]{1,0:T(8,128)(2,1)}, u32[]{:S(2)}) copy-start(bf16[1280,256]{1,0:T(8,128)(2,1)} %constant.66.clone.hl) | copy-start | bytes 1966084
  105.4 29.7 %copy-start.4 = (bf16[1280,256]{1,0:T(8,128)(2,1)S(1)}, bf16[1280,256]{1,0:T(8,128)(2,1)}, u32[]{:S(2)}) copy-start(bf16[1280,256]{1,0:T(8,128)(2,1)} %constant.65.clone.hh) | copy-start | bytes 1966084
  105.5 29.7 %copy-start.8 = (bf16[384,432]{1,0:T(8,128)(2,1)S(1)}, bf16[384,432]{1,0:T(8,128)(2,1)}, u32[]{:S(2)}) copy-start(bf16[384,432]{1,0:T(8,128)(2,1)} %constant.64.clone.wl) | copy-start | bytes 995332
  105.5 29.7 %copy-start.9 = (bf16[384,432]{1,0:T(8,128)(2,1)S(1)}, bf16[384,432]{1,0:T(8,128)(2,1)}, u32[]{:S(2)}) copy-start(bf16[384,432]{1,0:T(8,128)(2,1)} %constant.63.clone.wh) | copy-start | bytes 995332
  105.5 29.7 %copy-start.10 = (bf16[384,512]{1,0:T(8,128)(2,1)S(1)}, bf16[384,512]{1,0:T(8,128)(2,1)}, u32[]{:S(2)}) copy-start(bf16[384,512]{1,0:T(8,128)(2,1)} %constant.62.clone.vl) | copy-start | bytes 1179652
  105.5 29.7 %copy-start.14 = (s32[4096]{0:T(1024)S(1)}, s32[4096]{0:T(1024)}, u32[]{:S(2)}) copy-start(s32[4096]{0:T(1024)} %cells.3) | copy-start | bytes 49156
  105.5 29.7 %copy-start.15 = (f32[4096]{0:T(1024)S(1)}, f32[4096]{0:T(1024)}, u32[]{:S(2)}) copy-start(f32[4096]{0:T(1024)} %speed.3) | copy-start | bytes 49156
  109.4 6.6 %collective-permute-start.3 = (f32[280,384]{1,0:T(8,128)S(1)}, f32[280,384]{1,0:T(8,128)S(1)}, u32[]{:S(2)}, u32[]{:S(2)}) collective-permute-start(f32[280,384]{1,0:T(8,128)S(1)} %get-tuple-element.23), channel_id=1, source_target_pairs={{0,1},{1,0},{2,3},{3,2},{4,5},{5,4},{6,7},{7,6},{8,9},{9,8},{10,11... | collective-permute-start | bytes 1290248 | tf_op jit(solution)/shard_map/ppermute | solution.py:240
  114.3 11.5 %collective-permute-start.4 = (f32[280,384]{1,0:T(8,128)S(1)}, f32[280,384]{1,0:T(8,128)S(1)}, u32[]{:S(2)}, u32[]{:S(2)}) collective-permute-start(f32[280,384]{1,0:T(8,128)S(1)} %get-tuple-element.24), channel_id=1, source_target_pairs={{0,2},{1,3},{2,0},{3,1},{4,6},{5,7},{6,4},{7,5},{8,10},{9,11},{10,... | collective-permute-start | bytes 1290248 | tf_op jit(solution)/shard_map/ppermute | solution.py:240
  114.7 20.4 %collective-permute-start.5 = (f32[280,384]{1,0:T(8,128)S(1)}, f32[280,384]{1,0:T(8,128)S(1)}, u32[]{:S(2)}, u32[]{:S(2)}) collective-permute-start(f32[280,384]{1,0:T(8,128)S(1)} %get-tuple-element.25), channel_id=1, source_target_pairs={{0,3},{1,2},{2,1},{3,0},{4,7},{5,6},{6,5},{7,4},{8,11},{9,10},{10,... | collective-permute-start | bytes 1290248 | tf_op jit(solution)/shard_map/ppermute | solution.py:240
